TPU v7x, 256 devices: a whole 4x4x8 slice. The times are simulated.
256 devices in a mesh: context: 64 (over x, y, z_hi, core), tensor: 4 (over z_lo).
Axes of the slice: x: 4, y: 4, z: 8 (z_hi: 2, z_lo: 4; z = z_hi * 4 + z_lo), core: 2. Of those that a mesh axis runs over, the one named last changes fastest.
Arguments:
- tokens: bfloat16 [32768, 5120], P(('context', 'tensor')), may hold values from -6 to 6
- norm_gain: float32 [5120], replicated, may hold values from 0.1 to 1.9
- w_query: bfloat16 [5120, 4096], P('context', 'tensor'), may hold values from -0.078125 to 0.078125
- w_key: bfloat16 [5120, 512], P(None, 'tensor'), may hold values from -0.078125 to 0.078125
- w_value: bfloat16 [5120, 512], P(None, 'tensor'), may hold values from -0.078125 to 0.078125
- query_gain: float32 [128], replicated, may hold values from 1 to 8
- key_gain: float32 [128], replicated, may hold values from 1 to 8
- segments: int32 [32768], replicated, may hold values from 0 to 47, never falling along the last dimension, each value on 1 to 3072 neighbouring positions
- block_of: int32 [64], replicated, may hold values from 0 to 63, each once
Outputs:
- attended: bfloat16 [32768, 4096], P('context', 'tensor')
Inputs may be any that keep to these rules, and one draw needn't show every extreme that they name: `segments`: ids never fall along the sequence; each document has at most 3072 tokens and one has exactly 3072. `block_of`: a permutation of the 64 blocks of the sequence.
All inputs are finite; a program needn't handle non-finite values.
Results may differ from a plain program's by a relative error of at most 0.0065.
The roundings to bfloat16 on the way count: a program that leaves them out, or rounds other values in their place, can miss the bound.
Values may be sent and summed in bfloat16 or wider, within the bound.
A program may use at most 128 MiB of HBM per device.

v0:
```python
import math

import jax
import jax.numpy as jnp
from jax import lax
from jax.sharding import PartitionSpec as P


def yarn_frequencies(dim):
    theta = 1000000.0
    factor = 4.0
    initial = 32768.0
    lowest = math.floor(dim * math.log(initial / (32.0 * 2 * math.pi)) / (2 * math.log(theta)))
    highest = math.ceil(dim * math.log(initial / (1.0 * 2 * math.pi)) / (2 * math.log(theta)))
    lowest = max(lowest, 0)
    highest = min(highest, dim - 1)
    spread = max(highest - lowest, 0.001)
    result = []
    for index in range(dim // 2):
        base_freq = theta ** (-2.0 * index / dim)
        ramp = min(max((index - lowest) / spread, 0.0), 1.0)
        result.append(base_freq / factor * ramp + base_freq * (1.0 - ramp))
    return result


def rotate(values, offsets):
    dim = values.shape[-1]
    scale = 0.1 * math.log(4.0) + 1.0
    freqs = jnp.asarray(yarn_frequencies(dim), jnp.float32)
    angles = offsets.astype(jnp.float32)[:, None] * freqs[None, :]
    cosine = jnp.concatenate([jnp.cos(angles), jnp.cos(angles)], -1) * scale
    sine = jnp.concatenate([jnp.sin(angles), jnp.sin(angles)], -1) * scale
    half = dim // 2
    turned = jnp.concatenate([-values[..., half:], values[..., :half]], -1)
    return values * cosine[:, None, :] + turned * sine[:, None, :]


def head_norm(values, gain):
    return values * lax.rsqrt(jnp.mean(values * values, -1, keepdims=True) + 1e-06) * gain


def root_norm(rows, gain):
    widened = rows.astype(jnp.float32)
    return (
        widened * lax.rsqrt(jnp.mean(widened * widened, -1, keepdims=True) + 1e-06) * gain
    ).astype(jnp.bfloat16)


def shards(tokens, norm_gain, w_query, w_key, w_value, query_gain, key_gain, segments, block_of):
    normed = root_norm(lax.all_gather(tokens, "tensor", axis=0, tiled=True), norm_gain)
    length = normed.shape[0]
    head_size = query_gain.shape[0]
    kv_count = w_key.shape[1] // head_size
    q_count = w_query.shape[1] // head_size
    group = q_count // kv_count
    my_block = block_of[lax.axis_index("context")]
    places = my_block * length + jnp.arange(length, dtype=jnp.int32)
    doc_ids = lax.dynamic_slice_in_dim(segments, my_block * length, length, 0)
    offsets = places - jnp.searchsorted(segments, doc_ids, side="left")
    key = jnp.dot(normed, w_key, preferred_element_type=jnp.float32).reshape(
        length, kv_count, head_size
    )
    value = jnp.dot(normed, w_value, preferred_element_type=jnp.float32).astype(jnp.bfloat16)
    k_rot = (
        rotate(head_norm(key, key_gain), offsets)
        .astype(jnp.bfloat16)
        .reshape(length, kv_count * head_size)
    )
    stacked = jnp.concatenate([k_rot, value], 1)
    query = jnp.dot(
        normed,
        lax.all_gather(w_query, "context", axis=0, tiled=True),
        preferred_element_type=jnp.float32,
    )
    query = query.reshape(length, q_count, head_size)
    q_rot = rotate(head_norm(query, query_gain), offsets).astype(jnp.bfloat16)
    q_rot = q_rot.reshape(length, kv_count, group, head_size)
    first_id = segments[my_block * length]
    scale = head_size ** (-0.5)

    def tile(carry, block, other):
        last_id = segments[jnp.maximum(other, 0) * length + length - 1]
        needed = (other >= 0) & (other <= my_block) & (last_id >= first_id)

        def work(state):
            maxima, totals, weighted = state
            key_block = block[:, : kv_count * head_size].reshape(length, kv_count, head_size)
            value_block = block[:, kv_count * head_size :].reshape(length, kv_count, head_size)
            k_places = other * length + jnp.arange(length, dtype=jnp.int32)
            k_ids = lax.dynamic_slice_in_dim(segments, other * length, length, 0)
            allowed = (doc_ids[:, None] == k_ids[None, :]) & (k_places[None, :] <= places[:, None])
            scores = (
                jnp.einsum("qhgd,khd->hgqk", q_rot, key_block, preferred_element_type=jnp.float32)
                * scale
            )
            row_top = jnp.max(jnp.where(allowed, scores, -1e30), -1)
            new_top = jnp.maximum(maxima, row_top)
            weights = jnp.where(allowed, jnp.exp(scores - new_top[..., None]), 0.0)
            rescale = jnp.exp(maxima - new_top)
            totals = totals * rescale + jnp.sum(weights, -1)
            added = jnp.einsum(
                "hgqk,khd->hgqd",
                weights.astype(jnp.bfloat16),
                value_block,
                preferred_element_type=jnp.float32,
            )
            weighted = weighted * rescale[..., None] + added
            return (new_top, totals, weighted)

        return lax.cond(needed, work, lambda state: state, carry)

    start_state = (
        jnp.full((kv_count, group, length), -1e30, jnp.float32),
        jnp.zeros((kv_count, group, length), jnp.float32),
        jnp.zeros((kv_count, group, length, head_size), jnp.float32),
    )
    piece = lax.all_gather(stacked, "context", axis=0, tiled=True)
    count = piece.shape[0] // length

    def visit(index, inner):
        block = lax.dynamic_slice_in_dim(piece, index * length, length, 0)
        return tile(inner, block, block_of[index])

    state = lax.fori_loop(0, count, visit, start_state)
    result = state[2] / state[1][..., None]
    return result.transpose(2, 0, 1, 3).reshape(length, q_count * head_size).astype(jnp.bfloat16)


def solution(mesh):
    return jax.shard_map(
        shards,
        mesh=mesh,
        in_specs=(
            P(("context", "tensor"), None),
            P(),
            P("context", "tensor"),
            P(None, "tensor"),
            P(None, "tensor"),
            P(),
            P(),
            P(),
            P(),
        ),
        out_specs=P("context", "tensor"),
        check_vma=False,
    )
```

profile of v0, /device:TPU:20, one launch (start us, length us, event | category | flops | bytes accessed | tf_op | source)
XLA Modules:
  0.0 915.9 jit_solution(6607589387080954944)
XLA Ops:
  10.7 58.8 %while.47 = (s32[]{:T(128)}, u32[512]{0:T(512)S(1)}, u32[512]{0:T(512)S(1)}, s32[32768]{0:T(1024)}, s32[512]{0:T(512)S(1)}, /*index=5*/s32[]{:T(128)}, s32[]{:T(128)}, s32[]{}) while((s32[]{:T(128)}, u32[512]{0:T(512)S(1)}, u32[512]{0:T(512)S(1)}, s32[32768]{0:T(1024)}, s32[512]{0:T(512)S(1)}, /*index=5*/s32[]{:T(128)}, s32[]{:T(128)}, ...), condition=%wide.region_3.4_spmd.clone, body=%wide.region_2.3_spmd.clone.sunk | while | flops 10244 | bytes 40045 | solution.py:59
  25.4 3.6 gather_fusion
  36.4 3.6 gather_fusion
  43.8 3.6 gather_fusion
  70.1 43.1 %all-gather.4.cloned.1.call-done = bf16[512,5120]{1,0:T(8,128)(2,1)} async-done(((bf16[128,5120]{1,0:T(8,128)(2,1)}), bf16[512,5120]{1,0:T(8,128)(2,1)}) %all-gather.4.cloned.1.call-update) | async-done | bytes 5242896 | tf_op jit(solution)/shard_map/all_gather | solution.py:50
  113.2 3.7 fusion.19
  124.5 113.1 %all-gather.8.cloned.1.call-done = bf16[5120,1024]{1,0:T(8,128)(2,1)} async-done(((bf16[80,1024]{1,0:T(8,128)(2,1)}), bf16[5120,1024]{1,0:T(8,128)(2,1)}) %all-gather.8.cloned.1.call-update) | async-done | bytes 10485776 | tf_op jit(solution)/shard_map/all_gather | solution.py:72
  237.6 9.9 %fusion.33 = f32[512,1024]{1,0:T(8,128)S(1)} fusion(bf16[5120,1024]{1,0:T(8,128)(2,1)} %all-gather.8.cloned.1.call-done, bf16[512,5120]{1,0:T(8,128)(2,1)} %all-gather.4.cloned.1.call-done, f32[5120]{0:T(1024)S(1)} %copy-done.10, f32[512]{0:T(512)S(1)} %add_rsqrt_fusion.2), kind=kOutput, calls=%fused_computation.70 | convolution fusion | flops 5379194880 | bytes 17848320 | tf_op jit(solution)/shard_map/dot_general | solution.py:70
  254.3 156.5 %all-gather.6.cloned.1.call-done = bf16[32768,256]{0,1:T(8,128)(2,1)} async-done(((bf16[512,256]{0,1:T(8,128)(2,1)}), bf16[32768,256]{0,1:T(8,128)(2,1)}) %all-gather.6.cloned.1.call-update) | async-done | bytes 16777232 | tf_op jit(solution)/shard_map/all_gather | solution.py:117
  410.8 22.4 %copy.41 = bf16[32768,256]{1,0:T(8,128)(2,1)} copy(bf16[32768,256]{0,1:T(8,128)(2,1)} %all-gather.6.cloned.1.call-done) | data formatting | bytes 33554432
  433.3 473.4 %while.46 = (s32[]{:T(128)}, f32[1,8,512]{2,1,0:T(8,128)S(1)}, f32[1,8,512]{2,1,0:T(8,128)S(1)}, f32[1,8,512,128]{3,2,1,0:T(8,128)S(1)}, s32[64]{0:T(128)S(1)}, ...) while((s32[]{:T(128)}, f32[1,8,512]{2,1,0:T(8,128)S(1)}, ...), condition=%wide.region_10.11_spmd.clone, body=%wide.region_5.10_spmd.clone.sunk | while | flops 1098658816 | bytes 65557068 | solution.py:124
  445.0 15.0 %conditional.3 = ((f32[1,8,512]{2,1,0:T(8,128)S(1)}, f32[1,8,512]{2,1,0:T(8,128)S(1)}, f32[1,8,512,128]{3,2,1,0:T(8,128)S(1)})) conditional(s32[]{:T(128)} %convert_element_type.109, (f32[1,8,512]{2,1,0:T(8,128)S(1)}, f32[1,8,512]{2,1,0:T(8,128)S(1)}, f32[1,8,512,128]{3,2,1,0:T(8,128)S(1)}) %tuple.107, (s32[512]{0:T(512)S(1)}, s32[]{:T(128)}, ...), branch_computations={%region_6.6_spmd, %region_7.9_spmd} | conditional | flops 1098658816 | bytes 65554620 | solution.py:110
  446.7 5.6 fusion.2
  452.3 5.0 bitcast_add_fusion
  534.8 15.0 %conditional.3 = ((f32[1,8,512]{2,1,0:T(8,128)S(1)}, f32[1,8,512]{2,1,0:T(8,128)S(1)}, f32[1,8,512,128]{3,2,1,0:T(8,128)S(1)})) conditional(s32[]{:T(128)} %convert_element_type.109, (f32[1,8,512]{2,1,0:T(8,128)S(1)}, f32[1,8,512]{2,1,0:T(8,128)S(1)}, f32[1,8,512,128]{3,2,1,0:T(8,128)S(1)}) %tuple.107, (s32[512]{0:T(512)S(1)}, s32[]{:T(128)}, ...), branch_computations={%region_6.6_spmd, %region_7.9_spmd} | conditional | flops 1098658816 | bytes 65554620 | solution.py:110
  536.5 5.6 fusion.2
  542.1 5.0 bitcast_add_fusion
  555.5 15.0 %conditional.3 = ((f32[1,8,512]{2,1,0:T(8,128)S(1)}, f32[1,8,512]{2,1,0:T(8,128)S(1)}, f32[1,8,512,128]{3,2,1,0:T(8,128)S(1)})) conditional(s32[]{:T(128)} %convert_element_type.109, (f32[1,8,512]{2,1,0:T(8,128)S(1)}, f32[1,8,512]{2,1,0:T(8,128)S(1)}, f32[1,8,512,128]{3,2,1,0:T(8,128)S(1)}) %tuple.107, (s32[512]{0:T(512)S(1)}, s32[]{:T(128)}, ...), branch_computations={%region_6.6_spmd, %region_7.9_spmd} | conditional | flops 1098658816 | bytes 65554620 | solution.py:110
  557.2 5.6 fusion.2
  562.9 5.0 bitcast_add_fusion
  605.0 15.0 %conditional.3 = ((f32[1,8,512]{2,1,0:T(8,128)S(1)}, f32[1,8,512]{2,1,0:T(8,128)S(1)}, f32[1,8,512,128]{3,2,1,0:T(8,128)S(1)})) conditional(s32[]{:T(128)} %convert_element_type.109, (f32[1,8,512]{2,1,0:T(8,128)S(1)}, f32[1,8,512]{2,1,0:T(8,128)S(1)}, f32[1,8,512,128]{3,2,1,0:T(8,128)S(1)}) %tuple.107, (s32[512]{0:T(512)S(1)}, s32[]{:T(128)}, ...), branch_computations={%region_6.6_spmd, %region_7.9_spmd} | conditional | flops 1098658816 | bytes 65554620 | solution.py:110
  606.8 5.6 fusion.2
  612.4 5.0 bitcast_add_fusion
  729.3 15.0 %conditional.3 = ((f32[1,8,512]{2,1,0:T(8,128)S(1)}, f32[1,8,512]{2,1,0:T(8,128)S(1)}, f32[1,8,512,128]{3,2,1,0:T(8,128)S(1)})) conditional(s32[]{:T(128)} %convert_element_type.109, (f32[1,8,512]{2,1,0:T(8,128)S(1)}, f32[1,8,512]{2,1,0:T(8,128)S(1)}, f32[1,8,512,128]{3,2,1,0:T(8,128)S(1)}) %tuple.107, (s32[512]{0:T(512)S(1)}, s32[]{:T(128)}, ...), branch_computations={%region_6.6_spmd, %region_7.9_spmd} | conditional | flops 1098658816 | bytes 65554620 | solution.py:110
  731.1 5.6 fusion.2
  736.7 5.0 bitcast_add_fusion
  784.6 15.0 %conditional.3 = ((f32[1,8,512]{2,1,0:T(8,128)S(1)}, f32[1,8,512]{2,1,0:T(8,128)S(1)}, f32[1,8,512,128]{3,2,1,0:T(8,128)S(1)})) conditional(s32[]{:T(128)} %convert_element_type.109, (f32[1,8,512]{2,1,0:T(8,128)S(1)}, f32[1,8,512]{2,1,0:T(8,128)S(1)}, f32[1,8,512,128]{3,2,1,0:T(8,128)S(1)}) %tuple.107, (s32[512]{0:T(512)S(1)}, s32[]{:T(128)}, ...), branch_computations={%region_6.6_spmd, %region_7.9_spmd} | conditional | flops 1098658816 | bytes 65554620 | solution.py:110
  786.4 5.6 fusion.2
  792.0 5.0 bitcast_add_fusion
  851.4 15.0 %conditional.3 = ((f32[1,8,512]{2,1,0:T(8,128)S(1)}, f32[1,8,512]{2,1,0:T(8,128)S(1)}, f32[1,8,512,128]{3,2,1,0:T(8,128)S(1)})) conditional(s32[]{:T(128)} %convert_element_type.109, (f32[1,8,512]{2,1,0:T(8,128)S(1)}, f32[1,8,512]{2,1,0:T(8,128)S(1)}, f32[1,8,512,128]{3,2,1,0:T(8,128)S(1)}) %tuple.107, (s32[512]{0:T(512)S(1)}, s32[]{:T(128)}, ...), branch_computations={%region_6.6_spmd, %region_7.9_spmd} | conditional | flops 1098658816 | bytes 65554620 | solution.py:110
  853.1 5.6 fusion.2
  858.8 5.0 bitcast_add_fusion
  (463 shorter events, 218.8 us)
Async XLA Ops:
  6.5 110.4 %copy-start = (bf16[5120,128]{1,0:T(8,128)(2,1)S(1)}, bf16[5120,128]{1,0:T(8,128)(2,1)}, u32[]{:S(2)}) copy-start(bf16[5120,128]{1,0:T(8,128)(2,1)} %param.20) | copy-start | bytes 3932164
  6.5 106.7 %all-gather.4.cloned.1.call-start = ((), (), s32[]{:S(2)}) async-start(), calls=%async_computation | async-start | bytes 6553600 | tf_op jit(solution)/shard_map/all_gather | solution.py:50
  7.3 230.3 %all-gather.8.cloned.1.call-start = ((), (), s32[]{:S(2)}) async-start(), calls=%async_computation.2 | async-start | bytes 10649600 | tf_op jit(solution)/shard_map/all_gather | solution.py:72
  8.0 402.8 %all-gather.6.cloned.1.call-start = ((), (), s32[]{:S(2)}) async-start(), calls=%async_computation.1 | async-start | bytes 17039360 | tf_op jit(solution)/shard_map/all_gather | solution.py:117
  10.7 58.9 %copy-start.8 = (f32[64]{0:T(128)S(1)}, f32[64]{0:T(128)}, u32[]{:S(2)}) copy-start(f32[64]{0:T(128)} %constant.169.clone) | copy-start | bytes 772
  69.5 47.4 %copy-start.10 = (f32[5120]{0:T(1024)S(1)}, f32[5120]{0:T(1024)}, u32[]{:S(2)}) copy-start(f32[5120]{0:T(1024)} %param.18) | copy-start | bytes 61444
  113.2 4.0 copy-start.4
  117.2 2.0 copy-start.6
  117.2 2.3 copy-start.9
  247.5 1.3 copy-start.3
  247.5 2.5 copy-start.7
  252.1 1.0 copy-start.5
  254.3 179.0 %copy-start.11 = (s32[64]{0:T(128)S(1)}, s32[64]{0:T(128)}, u32[]{:S(2)}) copy-start(s32[64]{0:T(128)} %param.25) | copy-start | bytes 772
  452.3 5.9 copy-start.2
  542.1 5.9 copy-start.2
  562.9 5.9 copy-start.2
  612.4 5.9 copy-start.2
  736.7 5.9 copy-start.2
  792.0 5.9 copy-start.2
  858.8 5.9 copy-start.2
  906.7 2.7 copy-start.1
Sparse Core Ops, SparseCore 0:
  9.2 103.9 all-gather.3
  116.7 120.8 all-gather.7
  241.0 169.7 all-gather.5
where the time goes:
time: 923 us; the launch traced here: 916 us
  waiting for transfers between devices  314 us (34%)
  loops' own time  250 us (27%)
  local copies, waits for them, and re-layouts  224 us (24%)
  matrix products  88.3 us (10%)
  other arithmetic  25.4 us (3%)
  between operations  14 us (2%)
    another operation x1, loops' own time, shards(): state = lax.fori_loop(0, count, visit, start_state)  244 us
    all_gather x1, waiting for transfers between devices, shards(): piece = lax.all_gather(stacked, 'context', axis=0, tiled=True)  157 us
    all_gather x1, waiting for transfers between devices, shards(): lax.all_gather(w_query, 'context', axis=0, tiled=True)  113 us
    dynamic_slice x64, local copies, waits for them, and re-layouts, tile(): last_id = segments[jnp.maximum(other, 0) * length + length - 1]  86.3 us
    gather x16, local copies, waits for them, and re-layouts, shards(): offsets = places - jnp.searchsorted(segments, doc_ids, side='left')  57.5 us
    all_gather x1, waiting for transfers between devices, shards(): lax.all_gather(tokens, 'tensor', axis=0, tiled=True)  43.1 us
    dot_general x7, matrix products, work(): jnp.einsum('qhgd,khd->hgqk', q_rot, key_block, preferred_element_type=jnp...  39.3 us
    dynamic_slice x64, local copies, waits for them, and re-layouts, visit(): return tile(inner, block, block_of[index])  37.6 us
  transfers between devices with their start and end apart: 3, of which 3 were waited for; matrix products, arithmetic and copies ran while one was open for 9% of the time, Pallas kernels for 0%

commit v1 on v0

v1 whole, which is shorter than its diff:
```python
import functools
import math

import jax
import jax.numpy as jnp
from jax import lax
from jax.experimental import pallas as pl
from jax.experimental.pallas import tpu as pltpu
from jax.sharding import PartitionSpec as P

MESH = pl.DeviceIdType.MESH
BF16 = jnp.bfloat16
F32 = jnp.float32


def yarn_frequencies(dim):
    theta = 1000000.0
    factor = 4.0
    initial = 32768.0
    lowest = math.floor(dim * math.log(initial / (32.0 * 2 * math.pi)) / (2 * math.log(theta)))
    highest = math.ceil(dim * math.log(initial / (1.0 * 2 * math.pi)) / (2 * math.log(theta)))
    lowest = max(lowest, 0)
    highest = min(highest, dim - 1)
    spread = max(highest - lowest, 0.001)
    result = []
    for index in range(dim // 2):
        base_freq = theta ** (-2.0 * index / dim)
        ramp = min(max((index - lowest) / spread, 0.0), 1.0)
        result.append(base_freq / factor * ramp + base_freq * (1.0 - ramp))
    return result


def rotate(values, offsets):
    dim = values.shape[-1]
    scale = 0.1 * math.log(4.0) + 1.0
    freqs = jnp.asarray(yarn_frequencies(dim), jnp.float32)
    angles = offsets.astype(jnp.float32)[:, None] * freqs[None, :]
    cosine = jnp.concatenate([jnp.cos(angles), jnp.cos(angles)], -1) * scale
    sine = jnp.concatenate([jnp.sin(angles), jnp.sin(angles)], -1) * scale
    half = dim // 2
    turned = jnp.concatenate([-values[..., half:], values[..., :half]], -1)
    return values * cosine[:, None, :] + turned * sine[:, None, :]


def head_norm(values, gain):
    return values * lax.rsqrt(jnp.mean(values * values, -1, keepdims=True) + 1e-06) * gain


def root_norm(rows, gain):
    widened = rows.astype(jnp.float32)
    return (
        widened * lax.rsqrt(jnp.mean(widened * widened, -1, keepdims=True) + 1e-06) * gain
    ).astype(jnp.bfloat16)


def ctx_of(x, y, zh, k):
    return x * 16 + y * 4 + zh * 2 + k


def place():
    c = lax.axis_index("context")
    return c // 16, (c // 4) % 4, (c // 2) % 2, c % 2, lax.axis_index("tensor")


def gather_kernel(
    tok, wq, wk, wv,
    tok_all, wq_all, wk_all, wv_all,
    loc, tok_s, tok_r, w1_s, w1_r, zp_s, zp_r, zm_s, zm_r,
    yr_s, yr_r, yl_s, yl_r, fr_s, fr_r, fl_s, fl_r, co_s, co_r,
    kp_s, kp_r, km_s, km_r, kc_s, kc_r,
):
    x, y, zh, k, zl = place()
    me = ctx_of(x, y, zh, k)
    z = zh * 4 + zl
    d = (zl - x + 4) % 4
    zh_u = ((z - d + 8) % 8) // 4
    zh_d = 1 - zh_u

    def at_z(pos):
        pos = pos % 8
        return (ctx_of(x, y, pos // 4, k), pos % 4)

    up, down = at_z(z + 1), at_z(z + 7)
    x_dev = [(ctx_of((x + o) % 4, y, zh, k), zl) for o in range(4)]
    y_right, y_left = (ctx_of(x, (y + 1) % 4, zh, k), zl), (ctx_of(x, (y + 3) % 4, zh, k), zl)
    other = (ctx_of(x, y, zh, 1 - k), zl)

    barrier = pltpu.get_barrier_semaphore()
    for dev in (x_dev[1], x_dev[2], x_dev[3], up, down, y_right, y_left, other):
        pl.semaphore_signal(barrier, inc=1, device_id=dev, device_id_type=MESH)
    pl.semaphore_wait(barrier, 8)

    def remote(src, dst, ss, rs, dev):
        return pltpu.make_async_remote_copy(
            src_ref=src, dst_ref=dst, send_sem=ss, recv_sem=rs, device_id=dev, device_id_type=MESH
        )

    half = tok.shape[0] // 2
    halves = (pl.ds(0, half), pl.ds(half, half))

    def tok_copy(n, src, slot, part, dev):
        return remote(src, tok_all.at[slot, halves[part]], tok_s.at[n], tok_r.at[n], dev)

    sends = [
        tok_copy(0, tok.at[halves[0]], x, 0, x_dev[1]),
        tok_copy(3, tok.at[halves[1]], x, 1, x_dev[3]),
        tok_copy(1, tok.at[halves[1]], x, 1, x_dev[1]),
        tok_copy(2, tok.at[halves[0]], x, 0, x_dev[3]),
    ]
    w1_index = (x - zl + 4) % 4
    w1 = remote(wq, wq_all.at[me], w1_s.at[0], w1_r.at[w1_index], (ctx_of(zl, y, zh, k), zl))
    own_w = pltpu.make_async_copy(wq, wq_all.at[me], loc.at[1])

    @pl.when(d != 0)
    def _():
        w1.start()

    @pl.when(d == 0)
    def _():
        own_w.start()

    for copy in sends:
        copy.start()
    own_tok = pltpu.make_async_copy(tok, tok_all.at[x], loc.at[0])
    own_tok.start()
    own_k = pltpu.make_async_copy(wk, wk_all, loc.at[2])
    own_v = pltpu.make_async_copy(wv, wv_all, loc.at[3])

    @pl.when(d == 0)
    def _():
        own_k.start()
        own_v.start()

    def slot(i, zhalf, yy):
        return wq_all.at[ctx_of((x + i) % 4, yy, zhalf, k)]

    def zp(i):
        ref = slot(i, zh_u, y)
        return remote(ref, ref, zp_s.at[i], zp_r.at[i], up)

    def zm(i, zhalf):
        ref = slot(i, zhalf, y)
        return remote(ref, ref, zm_s.at[i], zm_r.at[i], down)

    def core(n, ref):
        return remote(ref, ref, co_s.at[n], co_r.at[n], other)

    def y_own(s, ref):
        return (
            remote(ref, ref, yr_s.at[s], yr_r.at[s], y_right),
            remote(ref, ref, yl_s.at[s], yl_r.at[s], y_left),
        )

    def fwd_right(i2, ref):
        return remote(ref, ref, fr_s.at[i2], fr_r.at[i2], y_right)

    def fwd_left(i2, ref):
        return remote(ref, ref, fl_s.at[i2], fl_r.at[i2], y_left)

    def spread(s, ref):
        right, left = y_own(s, ref)
        right.start()
        left.start()
        core(s, ref).start()

    def in_order(upper, lower):
        def step(t, carry):
            i = t - d

            @pl.when((i >= 0) & (i < 4))
            def _():
                upper(i)

            j = t - 4 + d

            @pl.when((j >= 0) & (j < 4))
            def _():
                lower(j)

            return carry

        lax.fori_loop(0, 8, step, 0)

    def z_upper(i):
        ref = slot(i, zh_u, y)

        @pl.when(d == 0)
        def _():
            @pl.when(i == 0)
            def _():
                own_w.wait()

            @pl.when(i != 0)
            def _():
                remote(ref, ref, w1_s.at[0], w1_r.at[i], other).wait_recv()

            zm(i, zh_u).start()

        @pl.when(d != 0)
        def _():
            zp(i).wait_recv()

        zp(i).start()
        spread(i, ref)

    def z_lower(i):
        ref = slot(i, zh_d, y)

        @pl.when(d == 0)
        def _():
            remote(ref, ref, zp_s.at[i], zp_r.at[i], up).wait_recv()

        @pl.when(d != 0)
        def _():
            zm(i, zh_d).wait_recv()

        @pl.when(d >= 2)
        def _():
            zm(i, zh_d).start()

        spread(4 + i, ref)

    in_order(z_upper, z_lower)

    left_x, right_x, far_x = (x + 3) % 4, (x + 1) % 4, (x + 2) % 4
    tok_copy(0, tok_all.at[left_x, halves[0]], left_x, 0, x_dev[1]).wait_recv()
    fwd_a = tok_copy(4, tok_all.at[left_x, halves[0]], left_x, 0, x_dev[1])
    fwd_a.start()
    tok_copy(3, tok_all.at[right_x, halves[1]], right_x, 1, x_dev[3]).wait_recv()
    fwd_b = tok_copy(5, tok_all.at[right_x, halves[1]], right_x, 1, x_dev[3])
    fwd_b.start()

    rows = wk.shape[0] // 8

    def part(i):
        return pl.ds((k * 4 + i) * rows, rows)

    def kv_core(n, ref):
        return remote(ref, ref, kc_s.at[n], kc_r.at[n], other)

    def kp(i, src):
        return remote(src.at[part(i)], wk_all.at[part(i)], kp_s.at[i], kp_r.at[i], up)

    def km(i, src):
        return remote(src.at[part(i)], wv_all.at[part(i)], km_s.at[i], km_r.at[i], down)

    y_l, y_r, y_far = (y + 3) % 4, (y + 1) % 4, (y + 2) % 4

    def ring(i, s, zhalf):
        ref = slot(i, zhalf, y_l)
        y_own(s, ref)[0].wait_recv()

        @pl.when(i % 2 == 0)
        def _():
            fwd_right(s // 2, ref).start()

        core(8 + s, ref).start()
        ref2 = slot(i, zhalf, y_r)
        y_own(s, ref2)[1].wait_recv()

        @pl.when(i % 2 == 1)
        def _():
            fwd_left(s // 2, ref2).start()

        core(16 + s, ref2).start()

    def kv_upper(i):
        @pl.when(d == 0)
        def _():
            kp(i, wk).start()
            km(i, wv).start()

        @pl.when(d != 0)
        def _():
            kp(i, wk_all).wait_recv()
            kv_core(i, wk_all.at[part(i)]).start()

        @pl.when((d == 1) | (d == 2))
        def _():
            kp(i, wk_all).start()

        ring(i, i, zh_u)

    def kv_lower(i):
        @pl.when(d != 0)
        def _():
            km(i, wv_all).wait_recv()
            kv_core(4 + i, wv_all.at[part(i)]).start()

        @pl.when(d >= 2)
        def _():
            km(i, wv_all).start()

        ring(i, 4 + i, zh_d)

    in_order(kv_upper, kv_lower)

    def far_upper(i):
        finish(i, i, zh_u)

    def far_lower(i):
        finish(i, 4 + i, zh_d)

    def finish(i, s, zhalf):
        ref = slot(i, zhalf, y_far)

        @pl.when(i % 2 == 0)
        def _():
            fwd_right(s // 2, ref).wait_recv()

        @pl.when(i % 2 == 1)
        def _():
            fwd_left(s // 2, ref).wait_recv()

        core(24 + s, ref).start()

    in_order(far_upper, far_lower)

    any_w = wq_all.at[me]

    def drain_core(n, carry):
        copy = core(n, any_w)
        copy.wait_send()
        copy.wait_recv()
        return carry

    lax.fori_loop(0, 32, drain_core, 0)

    def drain_y(s, carry):
        right, left = y_own(s, any_w)
        right.wait_send()
        left.wait_send()
        return carry

    lax.fori_loop(0, 8, drain_y, 0)

    def drain_four(i, carry):
        zp(i).wait_send()
        fwd_right(i, any_w).wait_send()
        fwd_left(i, any_w).wait_send()

        @pl.when((d == 0) | (d >= 2))
        def _():
            zm(i, zh_u).wait_send()
            km(i, wv_all).wait_send()

        @pl.when(d <= 2)
        def _():
            kp(i, wk_all).wait_send()

        @pl.when(d != 0)
        def _():
            for n, ref in ((i, wk_all), (4 + i, wv_all)):
                copy = kv_core(n, ref.at[part(i)])
                copy.wait_send()
                copy.wait_recv()

        return carry

    lax.fori_loop(0, 4, drain_four, 0)
    for copy in sends:
        copy.wait_send()
    fwd_a.wait_send()
    fwd_b.wait_send()
    tok_copy(1, tok_all.at[left_x, halves[1]], left_x, 1, x_dev[1]).wait_recv()
    tok_copy(2, tok_all.at[right_x, halves[0]], right_x, 0, x_dev[3]).wait_recv()
    tok_copy(4, tok_all.at[far_x, halves[0]], far_x, 0, x_dev[1]).wait_recv()
    tok_copy(5, tok_all.at[far_x, halves[1]], far_x, 1, x_dev[3]).wait_recv()
    own_tok.wait()

    @pl.when(d != 0)
    def _():
        w1.wait_send()

    @pl.when(d == 0)
    def _():
        own_k.wait()
        own_v.wait()


def gather(tokens, w_query, w_key, w_value):
    any_spec = pl.BlockSpec(memory_space=pl.ANY)
    dma = pltpu.SemaphoreType.DMA
    pair = lambda n: [dma((n,)), dma((n,))]
    return pl.pallas_call(
        gather_kernel,
        out_shape=(
            jax.ShapeDtypeStruct((4,) + tokens.shape, BF16),
            jax.ShapeDtypeStruct((64,) + w_query.shape, BF16),
            jax.ShapeDtypeStruct(w_key.shape, BF16),
            jax.ShapeDtypeStruct(w_value.shape, BF16),
        ),
        in_specs=[any_spec] * 4,
        out_specs=(any_spec,) * 4,
        scratch_shapes=[dma((4,))] + pair(6) + [dma((1,)), dma((4,))] + pair(4) + pair(4)
        + pair(8) + pair(8) + pair(4) + pair(4) + pair(32) + pair(4) + pair(4) + pair(8),
        compiler_params=pltpu.CompilerParams(collective_id=0, has_side_effects=True),
    )(tokens, w_query, w_key, w_value)


def exchange_kernel(
    table, q_in, kv_in,
    q_out, kv_all,
    qx, got, picked,
    loc, qx_s, qx_r, qz_s, qz_r, p1_s, p1_r, p2_s, p2_r,
):
    x, y, zh, k, zl = place()
    rest = y * 4 + zh * 2 + k
    mine = x * 8 + y * 2 + k
    barrier = pltpu.get_barrier_semaphore()

    def greet(dev):
        pl.semaphore_signal(barrier, inc=1, device_id=dev, device_id_type=MESH)

    for o in range(1, 4):
        greet((ctx_of((x + o) % 4, y, zh, k), zl))
        greet((ctx_of(x, y, zh, k), (zl + o) % 4))

    def greet_piece(r, carry):
        @pl.when((x != zl) | (r != rest))
        def _():
            greet((zl * 16 + r, x))

        return carry

    lax.fori_loop(0, 16, greet_piece, 0)

    def half_plane(d):
        return (ctx_of(d // 8, (d // 2) % 4, zh, d % 2), zl)

    def greet_plane(o, carry):
        greet(half_plane((mine + o) % 32))
        return carry

    lax.fori_loop(1, 32, greet_plane, 0)
    pl.semaphore_wait(barrier, 6 + 15 + 31 + ((x - zl + 4) % 4 + 3) // 4)

    def remote(src, dst, ss, rs, dev):
        return pltpu.make_async_remote_copy(
            src_ref=src, dst_ref=dst, send_sem=ss, recv_sem=rs, device_id=dev, device_id_type=MESH
        )

    def piece(r):
        p = (r // 4) * 2 + r % 2
        return remote(
            kv_in.at[p], got.at[pl.ds(rest * 4, 4)], p1_s.at[r], p1_r.at[rest], (zl * 16 + r, x)
        )

    own_piece = pltpu.make_async_copy(
        kv_in.at[(rest // 4) * 2 + rest % 2], got.at[pl.ds(rest * 4, 4)], loc.at[0]
    )

    def send_piece(o, carry):
        r = (rest + o) % 16

        @pl.when((x != zl) | (r != rest))
        def _():
            piece(r).start()

        return carry

    lax.fori_loop(0, 16, send_piece, 0)

    @pl.when(x == zl)
    def _():
        own_piece.start()

    def x_step(o):
        to = (x + o) % 4
        return remote(
            q_in.at[to], qx.at[x], qx_s.at[o], qx_r.at[o], (ctx_of(to, y, zh, k), zl)
        )

    for o in (1, 3, 2):
        x_step(o).start()

    def z_step(src, to):
        o = (to - zl + 4) % 4
        return remote(src, q_out.at[zl], qz_s.at[o], qz_r.at[o], (ctx_of(x, y, zh, k), to))

    def z_move(src, frm):
        @pl.when(frm != zl)
        def _():
            z_step(src, frm).start()

        @pl.when(frm == zl)
        def _():
            pltpu.make_async_copy(src, q_out.at[zl], loc.at[1]).start()

    z_move(q_in.at[x], x)

    def wait_piece(r, carry):
        @pl.when((x != zl) | (r != rest))
        def _():
            remote(
                kv_in.at[0], got.at[pl.ds(r * 4, 4)], p1_s.at[0], p1_r.at[r], (zl * 16 + r, x)
            ).wait_recv()

        return carry

    lax.fori_loop(0, 16, wait_piece, 0)

    @pl.when(x == zl)
    def _():
        own_piece.wait()

    def plane(d):
        return remote(
            picked.at[d], kv_all.at[:, :, mine], p2_s.at[d], p2_r.at[mine], half_plane(d)
        )

    def pick(d):
        for i in range(7):
            picked[d, :, i] = got[table[d, i]]

    def send_plane(o, carry):
        d = (mine + o) % 32
        pick(d)
        plane(d).start()
        return carry

    lax.fori_loop(1, 32, send_plane, 0)
    pick(mine)
    own_plane = pltpu.make_async_copy(picked.at[mine], kv_all.at[:, :, mine], loc.at[2])
    own_plane.start()

    for o in (1, 3, 2):
        frm = (x - o + 4) % 4
        remote(q_in.at[0], qx.at[frm], qx_s.at[o], qx_r.at[o], (ctx_of(frm, y, zh, k), zl)).wait_recv()
        z_move(qx.at[frm], frm)

    pltpu.make_async_copy(q_in.at[0], q_out.at[zl], loc.at[1]).wait()
    for o in (1, 2, 3):
        x_step(o).wait_send()
        z_step(q_in.at[0], (zl + o) % 4).wait_send()
        frm = (zl - o + 4) % 4
        remote(
            q_in.at[0], q_out.at[frm], qz_s.at[o], qz_r.at[o], (ctx_of(x, y, zh, k), frm)
        ).wait_recv()

    def drain_piece(r, carry):
        @pl.when((x != zl) | (r != rest))
        def _():
            piece(r).wait_send()

        return carry

    lax.fori_loop(0, 16, drain_piece, 0)
    own_plane.wait()

    def drain_plane(o, carry):
        d = (mine + o) % 32
        plane(d).wait_send()
        remote(
            picked.at[d], kv_all.at[:, :, d], p2_s.at[d], p2_r.at[d], half_plane(d)
        ).wait_recv()
        return carry

    lax.fori_loop(1, 32, drain_plane, 0)


def exchange(table, q_in, kv_in):
    any_spec = pl.BlockSpec(memory_space=pl.ANY)
    dma = pltpu.SemaphoreType.DMA
    pair = lambda n: [dma((n,)), dma((n,))]
    return pl.pallas_call(
        exchange_kernel,
        out_shape=(
            jax.ShapeDtypeStruct(q_in.shape, BF16),
            jax.ShapeDtypeStruct((2, 7, 32, 16, 128), BF16),
        ),
        in_specs=[pl.BlockSpec(memory_space=pltpu.SMEM), any_spec, any_spec],
        out_specs=(any_spec, any_spec),
        scratch_shapes=[
            pltpu.VMEM(q_in.shape, BF16),
            pltpu.VMEM((64, 2, 16, 128), BF16),
            pltpu.VMEM((32, 2, 7, 16, 128), BF16),
            dma((3,)),
        ] + pair(4) + pair(4) + pair(16) + pair(32),
        compiler_params=pltpu.CompilerParams(
            collective_id=1, has_side_effects=True, vmem_limit_bytes=16 << 20
        ),
    )(table, q_in, kv_in)


def attend_kernel(start_ref, q_ref, kv_ref, o_ref):
    length, head_size = q_ref.shape
    step = 256
    scale = head_size ** (-0.5) * math.log2(math.e)
    for r in range(length // step):
        rows = pl.ds(r * step, step)
        q = q_ref[rows, :]
        start = start_ref[rows, :]
        tiles = []
        top = None
        for i in range(7):
            scores = lax.dot_general(
                q, kv_ref[0, i], (((1,), (1,)), ((), ())), preferred_element_type=F32
            )
            at = lax.broadcasted_iota(jnp.int32, scores.shape, 1) + (i - 6) * length
            allowed = at >= start
            if i == 6:
                here = lax.broadcasted_iota(jnp.int32, scores.shape, 0) + r * step
                allowed = allowed & (at <= here)
            scores = jnp.where(allowed, scores, -1e30)
            tiles.append(scores)
            best = jnp.max(scores, -1, keepdims=True)
            top = best if top is None else jnp.maximum(top, best)
        total = None
        summed = None
        for i in range(7):
            weights = jnp.exp2((tiles[i] - top) * scale)
            added = jnp.sum(weights, -1, keepdims=True)
            part = jnp.dot(weights.astype(BF16), kv_ref[1, i], preferred_element_type=F32)
            total = added if total is None else total + added
            summed = part if summed is None else summed + part
        o_ref[rows, :] = (summed / total).astype(BF16)


def attend(start, q, kv):
    length, width = q.shape
    heads = width // 128
    return pl.pallas_call(
        attend_kernel,
        grid=(heads,),
        out_shape=jax.ShapeDtypeStruct(q.shape, BF16),
        in_specs=[
            pl.BlockSpec((length, 1), lambda h: (0, 0)),
            pl.BlockSpec((length, 128), lambda h: (0, h)),
            pl.BlockSpec(kv.shape, lambda h: (0, 0, 0, 0)),
        ],
        out_specs=pl.BlockSpec((length, 128), lambda h: (0, h)),
        compiler_params=pltpu.CompilerParams(vmem_limit_bytes=48 << 20),
    )(start, q, kv)


def shards(tokens, norm_gain, w_query, w_key, w_value, query_gain, key_gain, segments, block_of):
    x, y, zh, k, zl = place()
    rest = y * 4 + zh * 2 + k
    quarter = tokens.shape[0]
    length = quarter * 4
    tok_all, wq_all, wk_all, wv_all = gather(tokens, w_query, w_key, w_value)

    ids = jnp.arange(48, dtype=jnp.int32)
    starts = jnp.sum((segments[None, :] < ids[:, None]).astype(jnp.int32), 1)

    def start_of(at, size):
        doc = lax.dynamic_slice_in_dim(segments, at, size, 0)
        return jnp.sum(jnp.where(doc[:, None] == ids[None, :], starts[None, :], 0), 1)

    offsets = []
    for other in range(4):
        at = block_of[other * 16 + rest] * length + zl * quarter
        offsets.append(at + jnp.arange(quarter, dtype=jnp.int32) - start_of(at, quarter))
    offsets = jnp.concatenate(offsets)

    normed = root_norm(tok_all.reshape(length, -1), norm_gain)
    query = jnp.dot(normed, wq_all.reshape(normed.shape[1], -1), preferred_element_type=F32)
    key = jnp.dot(normed, wk_all, preferred_element_type=F32).reshape(length, 1, 128)
    value = jnp.dot(normed, wv_all, preferred_element_type=F32).astype(BF16)
    k_rot = rotate(head_norm(key, key_gain), offsets).astype(BF16)
    query = query.reshape(length, -1, 128)
    q_rot = rotate(head_norm(query, query_gain), offsets).astype(BF16)
    pieces = jnp.stack(
        [k_rot.reshape(4, 8, 16, 128), value.reshape(4, 8, 16, 128)], 2
    ).transpose(1, 0, 2, 3, 4)

    blocks = jnp.arange(64, dtype=jnp.int32)
    holder = jnp.sum(jnp.where(block_of[None, :] == blocks[:, None], blocks[None, :], 0), 1)
    d = jnp.arange(32, dtype=jnp.int32)
    wanted = block_of[ctx_of(d // 8, (d // 2) % 4, zh, d % 2)][:, None] - 6 + jnp.arange(7)[None, :]
    source = holder[jnp.maximum(wanted, 0)]
    table = (source % 16) * 4 + source // 16

    q_mine, kv = exchange(table, q_rot.reshape(4, quarter, -1), pieces)
    first = block_of[x * 16 + rest] * length
    start = (start_of(first, length) - first)[:, None]
    return attend(start, q_mine.reshape(length, -1), kv.reshape(2, 7, length, 128))


def solution(mesh):
    return jax.shard_map(
        shards,
        mesh=mesh,
        in_specs=(
            P(("context", "tensor"), None),
            P(),
            P("context", "tensor"),
            P(None, "tensor"),
            P(None, "tensor"),
            P(),
            P(),
            P(),
            P(),
        ),
        out_specs=P("context", "tensor"),
        check_vma=False,
    )
```

time: 923 us -> 289 us (0.31)
  the two profiles are of different devices: /device:TPU:20 before, /device:TPU:217 now
where the time goes in v1:
time: 289 us
  Pallas kernels  228 us (79%)
  local copies, waits for them, and re-layouts  23.7 us (8%)
  other arithmetic  17.6 us (6%)
  matrix products  16 us (6%)
  between operations  3.57 us (1%)
    pallas_call x1, Pallas kernels, exchange(): pl.pallas_call(exchange_kernel, out_shape=(jax.ShapeDtypeStruct(q_in.shap...  127 us
    pallas_call x1, Pallas kernels, gather(): pl.pallas_call(gather_kernel, out_shape=(jax.ShapeDtypeStruct((4,) + toke...  76.7 us
    pallas_call x1, Pallas kernels, attend(): pl.pallas_call(attend_kernel, grid=(heads,), out_shape=jax.ShapeDtypeStru...  24.1 us
    dot_general x1, local copies, waits for them, and re-layouts, shards(): jnp.dot(normed, wq_all.reshape(normed.shape[1], -1), preferred_element_ty...  13.9 us
    dot_general x1, matrix products, shards(): jnp.dot(normed, wq_all.reshape(normed.shape[1], -1), preferred_element_ty...  10.1 us
    convert_element_type x2, other arithmetic, root_norm(): return (widened * lax.rsqrt(jnp.mean(widened * widened, -1, keepdims=True...  8.8 us

profile of v1, /device:TPU:217, one launch (start us, length us, event | category | flops | bytes accessed | tf_op | source)
XLA Modules:
  0.0 288.7 jit_solution(544077287518068307)
XLA Ops:
  0.0 1.5 fusion.23
  4.1 0.8 fusion.22
  4.9 1.6 convert_reduce_fusion
  6.5 0.1 select_reduce_fusion.5
  6.7 1.2 multiply_cosine_fusion
  7.9 76.7 %shard_map.109 = (bf16[4,128,5120]{2,1,0:T(8,128)(2,1)}, bf16[64,80,1024]{2,1,0:T(8,128)(2,1)}, bf16[5120,128]{1,0:T(8,128)(2,1)}, bf16[5120,128]{1,0:T(8,128)(2,1)}) custom-call(bf16[128,5120]{1,0:T(8,128)(2,1)} %tok.1, bf16[80,1024]{1,0:T(8,128)(2,1)} %wq.1, bf16[5120,128]{1,0:T(8,128)(2,1)} %wk.1, bf16[5120,128]{1,0:T(8,128)(2,1)} %wv.1), custom_call_target="tpu_custom_call" | custom-call | tf_op jit(solution)/shard_map/pallas_call | solution.py:385
  84.6 3.7 %multiply_reduce_fusion = f32[4,128]{1,0:T(4,128)S(1)} fusion(bf16[4,128,5120]{2,1,0:T(8,128)(2,1)} %get-tuple-element.11), kind=kLoop, calls=%fused_computation.6 | loop fusion | flops 7863808 | bytes 5244928 | tf_op jit(solution)/shard_map/reduce_sum | solution.py:52
  88.3 0.3 copy-done.3
  88.6 2.0 fusion.1
  90.7 1.9 multiply_reduce_fusion.2
  92.7 0.2 copy-done.4
  92.9 0.1 fusion.5
  93.0 0.1 copy.22
  93.1 4.0 %convolution_convert_fusion = bf16[512,128]{1,0:T(8,128)(2,1)S(1)} fusion(bf16[512,5120]{1,0:T(8,128)(2,1)} %copy-done.4, bf16[5120,128]{1,0:T(8,128)(2,1)S(1)} %copy-done.9), kind=kOutput, calls=%fused_computation.14 | convolution fusion | flops 671154176 | bytes 6684672 | tf_op jit(solution)/shard_map/dot_general | solution.py:660
  97.2 6.8 %multiply_convert_fusion = bf16[4,128,5120]{2,1,0:T(8,128)(2,1)} fusion(f32[5120]{0:T(1024)S(1)} %copy-done.6, f32[4,128]{1,0:T(4,128)S(1)} %get-tuple-element.35, bf16[4,128,5120]{2,1,0:T(8,128)(2,1)} %get-tuple-element.11), kind=kLoop, calls=%fused_computation.5 | loop fusion | flops 10485760 | bytes 10508288 | tf_op jit(solution)/shard_map/convert_element_type | solution.py:53
  104.0 13.9 %copy.20 = bf16[1024,5120]{1,0:T(8,128)(2,1)} copy(bf16[1024,5120]{0,1:T(8,128)(2,1)} %bitcast.47) | data formatting | bytes 20971520 | tf_op jit(solution)/shard_map/dot_general | solution.py:658
  117.9 10.1 %multiply_reduce_fusion.1 = (f32[512,8]{0,1:T(8,128)S(1)}, f32[512,8,128]{0,2,1:T(8,128)S(1)}) fusion(bf16[512,5120,1]{1,0,2:T(8,128)(2,1)} %bitcast.49, bf16[8,128,5120]{2,1,0:T(8,128)(2,1)} %bitcast.48), kind=kOutput, calls=%fused_computation.13 | convolution fusion | flops 5369753600 | bytes 17842176 | tf_op jit(solution)/shard_map/dot_general | solution.py:658
  128.0 0.5 multiply_multiply_fusion
  128.5 0.2 slice_negate_fusion
  128.7 0.8 fusion.3
  129.5 0.3 reshape.384
  129.8 0.7 copy.26.q_in
  130.5 0.7 gather_fusion
  131.3 0.1 reshape.376
  131.4 0.1 select_reduce_fusion.1
  131.5 1.9 gather_fusion.1
  133.5 127.1 %shard_map.110 = (bf16[4,128,1024]{2,1,0:T(8,128)(2,1)S(1)}, bf16[2,7,32,16,128]{4,3,2,1,0:T(8,128)(2,1)S(1)}) custom-call(s32[32,7]{1,0:T(8,128)S(1)} %fusion.9.table, bf16[4,128,1024]{2,1,0:T(8,128)(2,1)S(1)} %copy.26.q_in, bf16[8,4,2,16,128]{4,3,2,1,0:T(8,128)(2,1)S(1)} %copy_bitcast_fusion.kv_in), custom_call_target="tpu_custom_call" | custom-call | tf_op jit(solution)/shard_map/pallas_call | solution.py:566
  260.7 1.0 copy-done
  262.3 0.8 dynamic_slice.31
  263.2 0.1 copy.25.start_ref
  263.4 1.2 copy-done.1
  264.6 24.1 %shard_map.111 = bf16[512,1024]{1,0:T(8,128)(2,1)} custom-call(s32[512,1]{1,0:T(8,128)S(1)} %copy.25.start_ref, bf16[512,1024]{1,0:T(8,128)(2,1)S(1)} %bitcast.46, bf16[2,7,512,128]{3,2,1,0:T(8,128)(2,1)S(1)} %bitcast.45), custom_call_target="tpu_custom_call" | custom-call | tf_op jit(solution)/shard_map/pallas_call | solution.py:623
  (34 shorter events, 0.6 us)
Async XLA Ops:
  0.0 88.3 %copy-start.6 = (f32[5120]{0:T(1024)S(1)}, f32[5120]{0:T(1024)}, u32[]{:S(2)}) copy-start(f32[5120]{0:T(1024)} %param.12) | copy-start | bytes 61444
  84.5 4.0 %copy-start.3 = (bf16[4,128,5120]{2,1,0:T(8,128)(2,1)S(1)}, bf16[4,128,5120]{2,1,0:T(8,128)(2,1)}, u32[]{:S(2)}) copy-start(bf16[4,128,5120]{2,1,0:T(8,128)(2,1)} %get-tuple-element.11) | copy-start | bytes 15728644
  88.6 2.1 copy-start.5
  90.6 2.2 copy-start.4
  90.6 1.9 copy-start.7
  90.7 2.5 copy-start.9
  117.9 10.1 %copy-start.8 = (f32[128]{0:T(128)S(1)}, f32[128]{0:T(128)}, u32[]{:S(2)}) copy-start(f32[128]{0:T(128)} %param.16) | copy-start | bytes 1540
  128.7 1.8 copy-start.2
  260.6 1.0 copy-start
  263.3 1.2 copy-start.1

commit v2 on v1

v2 whole, which is shorter than its diff:
```python
import math

import jax
import jax.numpy as jnp
from jax import lax
from jax.experimental import pallas as pl
from jax.experimental.pallas import tpu as pltpu
from jax.sharding import PartitionSpec as P

MESH = pl.DeviceIdType.MESH
BF16 = jnp.bfloat16
F32 = jnp.float32


def yarn_frequencies(dim):
    theta = 1000000.0
    factor = 4.0
    initial = 32768.0
    lowest = math.floor(dim * math.log(initial / (32.0 * 2 * math.pi)) / (2 * math.log(theta)))
    highest = math.ceil(dim * math.log(initial / (1.0 * 2 * math.pi)) / (2 * math.log(theta)))
    lowest = max(lowest, 0)
    highest = min(highest, dim - 1)
    spread = max(highest - lowest, 0.001)
    result = []
    for index in range(dim // 2):
        base_freq = theta ** (-2.0 * index / dim)
        ramp = min(max((index - lowest) / spread, 0.0), 1.0)
        result.append(base_freq / factor * ramp + base_freq * (1.0 - ramp))
    return result


def ctx_of(x, y, zh, k):
    return x * 16 + y * 4 + zh * 2 + k


def place():
    c = lax.axis_index("context")
    return c // 16, (c // 4) % 4, (c // 2) % 2, c % 2, lax.axis_index("tensor")


def front_kernel(
    table, tok, norm_gain, wq, wk, wv, q_gain, k_gain, cosine, sine,
    q_out, kv_all,
    tok_all, wq_all, wkv_all, q_send, qx, kv_send, got, picked,
    loc, tok_s, tok_r, w1_s, w1_r, zp_s, zp_r, zm_s, zm_r,
    yr_s, yr_r, yl_s, yl_r, fr_s, fr_r, fl_s, fl_r, co_s, co_r,
    kp_s, kp_r, km_s, km_r, kc_s, kc_r,
    qx_s, qx_r, qz_s, qz_r, p1_s, p1_r, p2_s, p2_r,
):
    x, y, zh, k, zl = place()
    me = ctx_of(x, y, zh, k)
    z = zh * 4 + zl
    d = (zl - x + 4) % 4
    zh_u = ((z - d + 8) % 8) // 4
    zh_d = 1 - zh_u

    def at_z(pos):
        pos = pos % 8
        return (ctx_of(x, y, pos // 4, k), pos % 4)

    up, down = at_z(z + 1), at_z(z + 7)
    x_dev = [(ctx_of((x + o) % 4, y, zh, k), zl) for o in range(4)]
    y_right, y_left = (ctx_of(x, (y + 1) % 4, zh, k), zl), (ctx_of(x, (y + 3) % 4, zh, k), zl)
    other = (ctx_of(x, y, zh, 1 - k), zl)

    rest = y * 4 + zh * 2 + k
    mine = x * 8 + y * 2 + k

    def half_plane(n):
        return (ctx_of(n // 8, (n // 2) % 4, zh, n % 2), zl)

    barrier = pltpu.get_barrier_semaphore()

    def greet(dev):
        pl.semaphore_signal(barrier, inc=1, device_id=dev, device_id_type=MESH)

    for dev in (x_dev[1], x_dev[2], x_dev[3], up, down, y_right, y_left, other):
        greet(dev)
    for o in range(1, 4):
        greet((me, (zl + o) % 4))

    def greet_piece(r, carry):
        @pl.when((x != zl) | (r != rest))
        def _():
            greet((zl * 16 + r, x))

        return carry

    lax.fori_loop(0, 16, greet_piece, 0)

    def greet_plane(o, carry):
        greet(half_plane((mine + o) % 32))
        return carry

    lax.fori_loop(1, 32, greet_plane, 0)

    quarter = tok.shape[0]
    width = tok.shape[1]

    def norm_rows(n, carry):
        rows = pl.ds(pl.multiple_of(n * 16, 16), 16)
        wide = tok[rows, :].astype(F32)
        mean = jnp.mean(wide * wide, -1, keepdims=True)
        wide = wide * lax.rsqrt(mean + 1e-06) * norm_gain[...]
        tok_all[pl.ds(pl.multiple_of(x * quarter + n * 16, 16), 16), :] = wide.astype(BF16)
        return carry

    lax.fori_loop(0, quarter // 16, norm_rows, 0)
    pl.semaphore_wait(barrier, 8 + 3 + 15 + 31 + ((x - zl + 4) % 4 + 3) // 4)

    def remote(src, dst, ss, rs, dev):
        return pltpu.make_async_remote_copy(
            src_ref=src, dst_ref=dst, send_sem=ss, recv_sem=rs, device_id=dev, device_id_type=MESH
        )

    half = quarter // 2

    def tok_copy(n, slot, part, dev):
        ref = tok_all.at[pl.ds(pl.multiple_of(slot * quarter + part * half, 16), half)]
        return remote(ref, ref, tok_s.at[n], tok_r.at[n], dev)

    def w_slot(c):
        return wq_all.at[pl.ds(pl.multiple_of(c * w_rows, 16), w_rows)]

    w_rows = wq.shape[0]
    sends = [
        tok_copy(0, x, 0, x_dev[1]),
        tok_copy(3, x, 1, x_dev[3]),
        tok_copy(1, x, 1, x_dev[1]),
        tok_copy(2, x, 0, x_dev[3]),
    ]
    w1_index = (x - zl + 4) % 4
    w1 = remote(wq, w_slot(me), w1_s.at[0], w1_r.at[w1_index], (ctx_of(zl, y, zh, k), zl))
    own_w = pltpu.make_async_copy(wq, w_slot(me), loc.at[1])

    @pl.when(d != 0)
    def _():
        w1.start()

    @pl.when(d == 0)
    def _():
        own_w.start()

    for copy in sends:
        copy.start()

    @pl.when(d == 0)
    def _():
        wkv_all[:, :128] = wk[...]
        wkv_all[:, 128:] = wv[...]

    def slot(i, zhalf, yy):
        return w_slot(ctx_of((x + i) % 4, yy, zhalf, k))

    def zp(i):
        ref = slot(i, zh_u, y)
        return remote(ref, ref, zp_s.at[i], zp_r.at[i], up)

    def zm(i, zhalf):
        ref = slot(i, zhalf, y)
        return remote(ref, ref, zm_s.at[i], zm_r.at[i], down)

    def core(n, ref):
        return remote(ref, ref, co_s.at[n], co_r.at[n], other)

    def y_own(s, ref):
        return (
            remote(ref, ref, yr_s.at[s], yr_r.at[s], y_right),
            remote(ref, ref, yl_s.at[s], yl_r.at[s], y_left),
        )

    def fwd_right(i2, ref):
        return remote(ref, ref, fr_s.at[i2], fr_r.at[i2], y_right)

    def fwd_left(i2, ref):
        return remote(ref, ref, fl_s.at[i2], fl_r.at[i2], y_left)

    def spread(s, ref):
        right, left = y_own(s, ref)
        right.start()
        left.start()
        core(s, ref).start()

    def in_order(upper, lower):
        def step(t, carry):
            i = t - d

            @pl.when((i >= 0) & (i < 4))
            def _():
                upper(i)

            j = t - 4 + d

            @pl.when((j >= 0) & (j < 4))
            def _():
                lower(j)

            return carry

        lax.fori_loop(0, 8, step, 0)

    def z_upper(i):
        ref = slot(i, zh_u, y)

        @pl.when(d == 0)
        def _():
            @pl.when(i == 0)
            def _():
                own_w.wait()

            @pl.when(i != 0)
            def _():
                remote(ref, ref, w1_s.at[0], w1_r.at[i], other).wait_recv()

            zm(i, zh_u).start()

        @pl.when(d != 0)
        def _():
            zp(i).wait_recv()

        zp(i).start()
        spread(i, ref)

    def z_lower(i):
        ref = slot(i, zh_d, y)

        @pl.when(d == 0)
        def _():
            remote(ref, ref, zp_s.at[i], zp_r.at[i], up).wait_recv()

        @pl.when(d != 0)
        def _():
            zm(i, zh_d).wait_recv()

        @pl.when(d >= 2)
        def _():
            zm(i, zh_d).start()

        spread(4 + i, ref)

    in_order(z_upper, z_lower)

    left_x, right_x, far_x = (x + 3) % 4, (x + 1) % 4, (x + 2) % 4
    tok_copy(0, left_x, 0, x_dev[1]).wait_recv()
    fwd_a = tok_copy(4, left_x, 0, x_dev[1])
    fwd_a.start()
    tok_copy(3, right_x, 1, x_dev[3]).wait_recv()
    fwd_b = tok_copy(5, right_x, 1, x_dev[3])
    fwd_b.start()

    rows = wk.shape[0] // 8

    def part(i):
        return pl.ds(pl.multiple_of((k * 4 + i) * rows, 16), rows)

    def key_part(i):
        return wkv_all.at[part(i), pl.ds(0, 128)]

    def value_part(i):
        return wkv_all.at[part(i), pl.ds(128, 128)]

    def kv_core(n, ref):
        return remote(ref, ref, kc_s.at[n], kc_r.at[n], other)

    def kp(i):
        return remote(key_part(i), key_part(i), kp_s.at[i], kp_r.at[i], up)

    def km(i):
        return remote(value_part(i), value_part(i), km_s.at[i], km_r.at[i], down)

    y_l, y_r, y_far = (y + 3) % 4, (y + 1) % 4, (y + 2) % 4

    def ring(i, s, zhalf):
        ref = slot(i, zhalf, y_l)
        y_own(s, ref)[0].wait_recv()

        @pl.when(i % 2 == 0)
        def _():
            fwd_right(s // 2, ref).start()

        core(8 + s, ref).start()
        ref2 = slot(i, zhalf, y_r)
        y_own(s, ref2)[1].wait_recv()

        @pl.when(i % 2 == 1)
        def _():
            fwd_left(s // 2, ref2).start()

        core(16 + s, ref2).start()

    def kv_upper(i):
        @pl.when(d == 0)
        def _():
            kp(i).start()
            km(i).start()

        @pl.when(d != 0)
        def _():
            kp(i).wait_recv()
            kv_core(i, key_part(i)).start()

        @pl.when((d == 1) | (d == 2))
        def _():
            kp(i).start()

        ring(i, i, zh_u)

    def kv_lower(i):
        @pl.when(d != 0)
        def _():
            km(i).wait_recv()
            kv_core(4 + i, value_part(i)).start()

        @pl.when(d >= 2)
        def _():
            km(i).start()

        ring(i, 4 + i, zh_d)

    in_order(kv_upper, kv_lower)

    tok_copy(1, left_x, 1, x_dev[1]).wait_recv()
    tok_copy(2, right_x, 0, x_dev[3]).wait_recv()
    tok_copy(4, far_x, 0, x_dev[1]).wait_recv()
    tok_copy(5, far_x, 1, x_dev[3]).wait_recv()

    @pl.when(d != 0)
    def _():
        def core_part(i, carry):
            kv_core(i, key_part(i)).wait_recv()
            kv_core(4 + i, value_part(i)).wait_recv()
            return carry

        lax.fori_loop(0, 4, core_part, 0)

    def turn(t, gain):
        t = t * lax.rsqrt(jnp.mean(t * t, -1, keepdims=True) + 1e-06) * gain[...]
        return (t * cosine[...] + pltpu.roll(t, 64, 1) * sine[...]).astype(BF16)

    both = jnp.dot(tok_all[...], wkv_all[...], preferred_element_type=F32)
    key = turn(both[:, :128], k_gain)
    value = both[:, 128:].astype(BF16)
    for p in range(8):
        for n in range(4):
            at = n * 128 + p * 16
            kv_send[p, n, 0] = key[at : at + 16]
            kv_send[p, n, 1] = value[at : at + 16]

    def piece(r):
        p = (r // 4) * 2 + r % 2
        return remote(
            kv_send.at[p], got.at[pl.ds(rest * 4, 4)], p1_s.at[r], p1_r.at[rest], (zl * 16 + r, x)
        )

    own_piece = pltpu.make_async_copy(
        kv_send.at[(rest // 4) * 2 + rest % 2], got.at[pl.ds(rest * 4, 4)], loc.at[0]
    )

    def send_piece(o, carry):
        r = (rest + o) % 16

        @pl.when((x != zl) | (r != rest))
        def _():
            piece(r).start()

        return carry

    lax.fori_loop(0, 16, send_piece, 0)

    @pl.when(x == zl)
    def _():
        own_piece.start()

    def far_upper(i):
        finish(i, i, zh_u)

    def far_lower(i):
        finish(i, 4 + i, zh_d)

    def finish(i, s, zhalf):
        ref = slot(i, zhalf, y_far)

        @pl.when(i % 2 == 0)
        def _():
            fwd_right(s // 2, ref).wait_recv()

        @pl.when(i % 2 == 1)
        def _():
            fwd_left(s // 2, ref).wait_recv()

        core(24 + s, ref).start()

    in_order(far_upper, far_lower)

    any_w = w_slot(me)

    def wait_core(n, carry):
        core(n, any_w).wait_recv()
        return carry

    lax.fori_loop(0, 32, wait_core, 0)

    def wait_piece(r, carry):
        @pl.when((x != zl) | (r != rest))
        def _():
            remote(
                kv_send.at[0], got.at[pl.ds(r * 4, 4)], p1_s.at[0], p1_r.at[r], (zl * 16 + r, x)
            ).wait_recv()

        return carry

    lax.fori_loop(0, 16, wait_piece, 0)

    @pl.when(x == zl)
    def _():
        own_piece.wait()

    def plane(n):
        return remote(
            picked.at[n], kv_all.at[:, :, mine], p2_s.at[n], p2_r.at[mine], half_plane(n)
        )

    def pick(n):
        for i in range(7):
            picked[n, :, i] = got[table[n, i]]

    def send_plane(o, carry):
        n = (mine + o) % 32
        pick(n)
        plane(n).start()
        return carry

    lax.fori_loop(1, 32, send_plane, 0)
    pick(mine)
    own_plane = pltpu.make_async_copy(picked.at[mine], kv_all.at[:, :, mine], loc.at[2])
    own_plane.start()

    def heads(n):
        return pl.ds(n * 2, 2)

    def x_step(n, o):
        to = (x + o) % 4
        return remote(
            q_send.at[heads(n), to], qx.at[heads(n), x], qx_s.at[n, o], qx_r.at[n, o],
            (ctx_of(to, y, zh, k), zl),
        )

    def z_step(n, src, to):
        o = (to - zl + 4) % 4
        return remote(
            src.at[heads(n), to], q_out.at[heads(n), zl], qz_s.at[n, o], qz_r.at[n, o], (me, to)
        )

    def z_move(n, src, frm):
        @pl.when(frm != zl)
        def _():
            z_step(n, src, frm).start()

        @pl.when(frm == zl)
        def _():
            pltpu.make_async_copy(
                src.at[heads(n), frm], q_out.at[heads(n), zl], loc.at[3 + n]
            ).start()

    def project(n, carry):
        columns = pl.ds(pl.multiple_of(n * 256, 256), 256)
        both = jnp.dot(tok_all[...], wq_all[:, columns], preferred_element_type=F32)
        for h in range(2):
            head = turn(both[:, h * 128 : h * 128 + 128], q_gain)
            q_send[n * 2 + h] = head.reshape(4, quarter, 128)
        for o in (1, 3, 2):
            x_step(n, o).start()
        z_move(n, q_send, x)
        return carry

    lax.fori_loop(0, 4, project, 0)

    def pass_on(n, carry):
        for o in (1, 3, 2):
            frm = (x - o + 4) % 4
            remote(
                q_send.at[heads(n), 0], qx.at[heads(n), frm], qx_s.at[n, o], qx_r.at[n, o],
                (ctx_of(frm, y, zh, k), zl),
            ).wait_recv()
            z_move(n, qx, frm)
        return carry

    lax.fori_loop(0, 4, pass_on, 0)

    def drain_q(n, carry):
        pltpu.make_async_copy(
            q_send.at[heads(n), 0], q_out.at[heads(n), zl], loc.at[3 + n]
        ).wait()
        for o in (1, 2, 3):
            x_step(n, o).wait_send()
            z_step(n, q_send, (zl + o) % 4).wait_send()
            frm = (zl - o + 4) % 4
            remote(
                q_send.at[heads(n), 0], q_out.at[heads(n), frm], qz_s.at[n, o], qz_r.at[n, o],
                (me, frm),
            ).wait_recv()
        return carry

    lax.fori_loop(0, 4, drain_q, 0)

    def drain_piece(r, carry):
        @pl.when((x != zl) | (r != rest))
        def _():
            piece(r).wait_send()

        return carry

    lax.fori_loop(0, 16, drain_piece, 0)
    own_plane.wait()

    def drain_plane(o, carry):
        n = (mine + o) % 32
        plane(n).wait_send()
        remote(
            picked.at[n], kv_all.at[:, :, n], p2_s.at[n], p2_r.at[n], half_plane(n)
        ).wait_recv()
        return carry

    lax.fori_loop(1, 32, drain_plane, 0)

    def drain_core(n, carry):
        core(n, any_w).wait_send()
        return carry

    lax.fori_loop(0, 32, drain_core, 0)

    def drain_y(s, carry):
        right, left = y_own(s, any_w)
        right.wait_send()
        left.wait_send()
        return carry

    lax.fori_loop(0, 8, drain_y, 0)

    def drain_four(i, carry):
        zp(i).wait_send()
        fwd_right(i, any_w).wait_send()
        fwd_left(i, any_w).wait_send()

        @pl.when((d == 0) | (d >= 2))
        def _():
            zm(i, zh_u).wait_send()
            km(i).wait_send()

        @pl.when(d <= 2)
        def _():
            kp(i).wait_send()

        @pl.when(d != 0)
        def _():
            kv_core(i, key_part(i)).wait_send()
            kv_core(4 + i, value_part(i)).wait_send()

        return carry

    lax.fori_loop(0, 4, drain_four, 0)
    for copy in sends:
        copy.wait_send()
    fwd_a.wait_send()
    fwd_b.wait_send()

    @pl.when(d != 0)
    def _():
        w1.wait_send()


def front(table, tokens, norm_gain, w_query, w_key, w_value, q_gain, k_gain, cosine, sine):
    vmem = pl.BlockSpec(memory_space=pltpu.VMEM)
    hbm = pl.BlockSpec(memory_space=pl.ANY)
    dma = pltpu.SemaphoreType.DMA
    pair = lambda *n: [dma(n), dma(n)]
    rows, width = tokens.shape
    columns = w_query.shape[1]
    flops = 2 * 4 * rows * width * (columns + 256)
    return pl.pallas_call(
        front_kernel,
        out_shape=(
            jax.ShapeDtypeStruct((8, 4, rows, 128), BF16),
            jax.ShapeDtypeStruct((2, 7, 32, 16, 128), BF16),
        ),
        in_specs=[pl.BlockSpec(memory_space=pltpu.SMEM)] + [vmem] * 9,
        out_specs=(hbm, hbm),
        scratch_shapes=[
            pltpu.VMEM((4 * rows, width), BF16),
            pltpu.VMEM((width, columns), BF16),
            pltpu.VMEM((width, 256), BF16),
            pltpu.VMEM((8, 4, rows, 128), BF16),
            pltpu.VMEM((8, 4, rows, 128), BF16),
            pltpu.VMEM((8, 4, 2, 16, 128), BF16),
            pltpu.VMEM((64, 2, 16, 128), BF16),
            pltpu.VMEM((32, 2, 7, 16, 128), BF16),
            dma((7,)),
        ] + pair(6) + [dma((1,)), dma((4,))] + pair(4) + pair(4) + pair(8) + pair(8)
        + pair(4) + pair(4) + pair(32) + pair(4) + pair(4) + pair(8)
        + pair(4, 4) + pair(4, 4) + pair(16) + pair(32),
        cost_estimate=pl.CostEstimate(flops=flops, bytes_accessed=10 << 20, transcendentals=0),
        compiler_params=pltpu.CompilerParams(
            collective_id=0, has_side_effects=True, vmem_limit_bytes=50 << 20
        ),
    )(table, tokens, norm_gain, w_query, w_key, w_value, q_gain, k_gain, cosine, sine)


def attend_kernel(start_ref, q_ref, kv_ref, o_ref):
    _, length, head_size = q_ref.shape
    step = 256
    scale = head_size ** (-0.5) * math.log2(math.e)
    for r in range(length // step):
        rows = pl.ds(r * step, step)
        q = q_ref[0, rows, :]
        start = start_ref[rows, :]
        tiles = []
        top = None
        for i in range(7):
            scores = lax.dot_general(
                q, kv_ref[0, i], (((1,), (1,)), ((), ())), preferred_element_type=F32
            )
            at = lax.broadcasted_iota(jnp.int32, scores.shape, 1) + (i - 6) * length
            allowed = at >= start
            if i == 6:
                here = lax.broadcasted_iota(jnp.int32, scores.shape, 0) + r * step
                allowed = allowed & (at <= here)
            scores = jnp.where(allowed, scores, -1e30)
            tiles.append(scores)
            best = jnp.max(scores, -1, keepdims=True)
            top = best if top is None else jnp.maximum(top, best)
        total = None
        summed = None
        for i in range(7):
            weights = jnp.exp2((tiles[i] - top) * scale)
            added = jnp.sum(weights, -1, keepdims=True)
            part = jnp.dot(weights.astype(BF16), kv_ref[1, i], preferred_element_type=F32)
            total = added if total is None else total + added
            summed = part if summed is None else summed + part
        o_ref[rows, :] = (summed / total).astype(BF16)


def attend(start, q, kv):
    heads, length, size = q.shape
    return pl.pallas_call(
        attend_kernel,
        grid=(heads,),
        out_shape=jax.ShapeDtypeStruct((length, heads * size), BF16),
        in_specs=[
            pl.BlockSpec((length, 1), lambda h: (0, 0)),
            pl.BlockSpec((1, length, size), lambda h: (h, 0, 0)),
            pl.BlockSpec(kv.shape, lambda h: (0, 0, 0, 0)),
        ],
        out_specs=pl.BlockSpec((length, size), lambda h: (0, h)),
        compiler_params=pltpu.CompilerParams(vmem_limit_bytes=48 << 20),
    )(start, q, kv)


def shards(tokens, norm_gain, w_query, w_key, w_value, query_gain, key_gain, segments, block_of):
    x, y, zh, k, zl = place()
    rest = y * 4 + zh * 2 + k
    quarter = tokens.shape[0]
    length = quarter * 4

    ids = jnp.arange(48, dtype=jnp.int32)
    starts = jnp.sum((segments[None, :] < ids[:, None]).astype(jnp.int32), 1)

    def start_of(at, size):
        doc = lax.dynamic_slice_in_dim(segments, at, size, 0)
        return jnp.sum(jnp.where(doc[:, None] == ids[None, :], starts[None, :], 0), 1)

    offsets = []
    for other in range(4):
        at = block_of[other * 16 + rest] * length + zl * quarter
        offsets.append(at + jnp.arange(quarter, dtype=jnp.int32) - start_of(at, quarter))
    offsets = jnp.concatenate(offsets)

    angles = offsets.astype(F32)[:, None] * jnp.asarray(yarn_frequencies(128), F32)[None, :]
    scale = 0.1 * math.log(4.0) + 1.0
    cosine, sine = jnp.cos(angles) * scale, jnp.sin(angles) * scale
    cosine = jnp.concatenate([cosine, cosine], -1)
    sine = jnp.concatenate([-sine, sine], -1)

    blocks = jnp.arange(64, dtype=jnp.int32)
    holder = jnp.sum(jnp.where(block_of[None, :] == blocks[:, None], blocks[None, :], 0), 1)
    d = jnp.arange(32, dtype=jnp.int32)
    wanted = block_of[ctx_of(d // 8, (d // 2) % 4, zh, d % 2)][:, None] - 6 + jnp.arange(7)[None, :]
    source = holder[jnp.maximum(wanted, 0)]
    table = (source % 16) * 4 + source // 16

    q_mine, kv = front(
        table, tokens, norm_gain[None, :], w_query, w_key, w_value,
        query_gain[None, :], key_gain[None, :], cosine, sine,
    )
    first = block_of[x * 16 + rest] * length
    start = (start_of(first, length) - first)[:, None]
    return attend(start, q_mine.reshape(8, length, 128), kv.reshape(2, 7, length, 128))


def solution(mesh):
    return jax.shard_map(
        shards,
        mesh=mesh,
        in_specs=(
            P(("context", "tensor"), None),
            P(),
            P("context", "tensor"),
            P(None, "tensor"),
            P(None, "tensor"),
            P(),
            P(),
            P(),
            P(),
        ),
        out_specs=P("context", "tensor"),
        check_vma=False,
    )
```

time: 289 us -> 204 us (0.71)
  the two profiles are of different devices: /device:TPU:217 before, /device:TPU:6 now
where the time goes in v2:
time: 204 us; the launch traced here: 203 us
  Pallas kernels  188 us (92%)
  local copies, waits for them, and re-layouts  8.22 us (4%)
  other arithmetic  4.02 us (2%)
  between operations  3.4 us (2%)
    pallas_call x1, Pallas kernels, front(): pl.pallas_call(front_kernel, out_shape=(jax.ShapeDtypeStruct((8, 4, rows,...  164 us
    pallas_call x1, Pallas kernels, attend(): pl.pallas_call(attend_kernel, grid=(heads,), out_shape=jax.ShapeDtypeStru...  23.9 us

profile of v2, /device:TPU:6, one launch (start us, length us, event | category | flops | bytes accessed | tf_op | source)
XLA Modules:
  0.0 203.4 jit_solution(8341249141492613585)
XLA Ops:
  0.0 1.5 fusion.17
  4.7 0.8 fusion.16
  5.6 1.6 convert_reduce_fusion
  7.2 0.1 select_reduce_fusion.5
  7.3 0.8 select_reduce_fusion.1
  8.1 0.8 dynamic_slice.31
  8.9 0.1 select_reduce_fusion
  9.0 1.4 gather_fusion
  10.3 0.1 add_maximum_fusion
  10.4 0.1 reshape.242
  10.5 0.0 copy-start.6
  10.5 1.9 gather_fusion.1
  12.4 0.0 copy-start.1
  12.4 0.0 copy-start.2
  12.4 0.0 copy-start.3
  12.5 0.0 copy-start.4
  12.5 0.0 copy-start.5
  12.5 0.1 reshape.241
  12.6 0.1 copy.12.start_ref
  12.8 0.0 copy-done.6
  12.8 1.0 fusion.2
  13.8 0.1 pad_maximum_fusion.1.sine
  13.9 0.1 pad_maximum_fusion.cosine
  14.1 0.0 copy-done.1
  14.1 0.0 copy-done.2
  14.1 0.0 copy-done.3
  14.1 0.0 copy-done.4
  14.1 0.0 copy-done.5
  14.1 163.9 %shard_map.100 = (bf16[8,4,128,128]{3,2,1,0:T(8,128)(2,1)S(1)}, bf16[2,7,32,16,128]{4,3,2,1,0:T(8,128)(2,1)}) custom-call(s32[32,7]{1,0:T(8,128)S(1)} %fusion.4.table, bf16[128,5120]{1,0:T(8,128)(2,1)S(1)} %copy-done.1, f32[1,5120]{1,0:T(1,128)S(1)} %bitcast.17, bf16[80,1024]{1,0:T(8,128)(2,1)S(1)} %copy-done.2, bf16[5120,128]{1,0:T(8,128)(2,1)} %wk.1, ...), custom_call_target="tpu_custom_call" | custom-call | flops 6710886400 | bytes 10485760 | tf_op jit(solution)/shard_map/pallas_call | solution.py:580
  178.0 0.0 copy-start
  178.0 1.5 copy-done
  179.5 23.9 %shard_map.101 = bf16[512,1024]{1,0:T(8,128)(2,1)} custom-call(s32[512,1]{1,0:T(8,128)S(1)} %copy.12.start_ref, bf16[8,512,128]{2,1,0:T(8,128)(2,1)S(1)} %bitcast.16, bf16[2,7,512,128]{3,2,1,0:T(8,128)(2,1)S(1)} %bitcast.15), custom_call_target="tpu_custom_call" | custom-call | tf_op jit(solution)/shard_map/pallas_call | solution.py:644
  (9 shorter events, 0.1 us)
Async XLA Ops:
  10.5 2.2 %copy-start.6 = (f32[64]{0:T(128)S(1)}, f32[64]{0:T(128)}, u32[]{:S(2)}) copy-start(f32[64]{0:T(128)} %constant.162.clone) | copy-start | bytes 772
  12.4 1.7 copy-start.1
  12.4 1.7 copy-start.2
  12.4 1.7 copy-start.3
  12.5 1.6 copy-start.4
  12.5 1.6 copy-start.5
  178.0 1.5 copy-start

commit v3 on v2

--- a/solution.py
+++ b/solution.py
@@ -10,6 +10,11 @@
 MESH = pl.DeviceIdType.MESH
 BF16 = jnp.bfloat16
 F32 = jnp.float32
+STEPS = (
+    (1, 0), (0, 1), (3, 0), (0, 3), (1, 1), (3, 3), (1, 3), (3, 1),
+    (2, 0), (0, 2), (2, 1), (1, 2), (2, 3), (3, 2), (2, 2),
+)
+PLACES = ((0, 0, 1),) + tuple((dx, dy, dk) for dk in (0, 1) for dx, dy in STEPS)
 
 
 def yarn_frequencies(dim):
@@ -400,41 +405,6 @@
 
     lax.fori_loop(0, 32, wait_core, 0)
 
-    def wait_piece(r, carry):
-        @pl.when((x != zl) | (r != rest))
-        def _():
-            remote(
-                kv_send.at[0], got.at[pl.ds(r * 4, 4)], p1_s.at[0], p1_r.at[r], (zl * 16 + r, x)
-            ).wait_recv()
-
-        return carry
-
-    lax.fori_loop(0, 16, wait_piece, 0)
-
-    @pl.when(x == zl)
-    def _():
-        own_piece.wait()
-
-    def plane(n):
-        return remote(
-            picked.at[n], kv_all.at[:, :, mine], p2_s.at[n], p2_r.at[mine], half_plane(n)
-        )
-
-    def pick(n):
-        for i in range(7):
-            picked[n, :, i] = got[table[n, i]]
-
-    def send_plane(o, carry):
-        n = (mine + o) % 32
-        pick(n)
-        plane(n).start()
-        return carry
-
-    lax.fori_loop(1, 32, send_plane, 0)
-    pick(mine)
-    own_plane = pltpu.make_async_copy(picked.at[mine], kv_all.at[:, :, mine], loc.at[2])
-    own_plane.start()
-
     def heads(n):
         return pl.ds(n * 2, 2)
 
@@ -474,6 +444,38 @@
         return carry
 
     lax.fori_loop(0, 4, project, 0)
+
+    def wait_piece(r, carry):
+        @pl.when((x != zl) | (r != rest))
+        def _():
+            remote(
+                kv_send.at[0], got.at[pl.ds(r * 4, 4)], p1_s.at[0], p1_r.at[r], (zl * 16 + r, x)
+            ).wait_recv()
+
+        return carry
+
+    lax.fori_loop(0, 16, wait_piece, 0)
+
+    @pl.when(x == zl)
+    def _():
+        own_piece.wait()
+
+    def plane(n):
+        return remote(
+            picked.at[n], kv_all.at[:, :, mine], p2_s.at[n], p2_r.at[mine], half_plane(n)
+        )
+
+    def pick(n):
+        for i in range(7):
+            picked[n, :, i] = got[table[n, i]]
+
+    for dx, dy, dk in PLACES:
+        n = ((x + dx) % 4) * 8 + ((y + dy) % 4) * 2 + (k + dk) % 2
+        pick(n)
+        plane(n).start()
+    pick(mine)
+    own_plane = pltpu.make_async_copy(picked.at[mine], kv_all.at[:, :, mine], loc.at[2])
+    own_plane.start()
 
     def pass_on(n, carry):
         for o in (1, 3, 2):

time: 204 us -> 178 us (0.87)
  the two profiles are of different devices: /device:TPU:6 before, /device:TPU:7 now
where the time goes in v3:
time: 178 us
  Pallas kernels  162 us (91%)
  local copies, waits for them, and re-layouts  8.22 us (5%)
  other arithmetic  4.02 us (2%)
  between operations  3.4 us (2%)
    pallas_call x1, Pallas kernels, front(): pl.pallas_call(front_kernel, out_shape=(jax.ShapeDtypeStruct((8, 4, rows,...  138 us
    pallas_call x1, Pallas kernels, attend(): pl.pallas_call(attend_kernel, grid=(heads,), out_shape=jax.ShapeDtypeStru...  23.9 us

profile of v3, /device:TPU:7, one launch (start us, length us, event | category | flops | bytes accessed | tf_op | source)
XLA Modules:
  0.0 177.5 jit_solution(18184371261766974991)
XLA Ops:
  0.0 1.5 fusion.17
  4.7 0.8 fusion.16
  5.6 1.6 convert_reduce_fusion
  7.2 0.1 select_reduce_fusion.5
  7.3 0.8 select_reduce_fusion.1
  8.1 0.8 dynamic_slice.31
  8.9 0.1 select_reduce_fusion
  9.0 1.4 gather_fusion
  10.3 0.1 add_maximum_fusion
  10.4 0.1 reshape.242
  10.5 0.0 copy-start.6
  10.5 1.9 %gather_fusion.1 = s32[224]{0:T(256)S(1)} fusion(s32[64]{0:T(128)S(1)} %select_reduce_fusion.1, s32[1024]{0:T(1024)S(1)} %pad_clamp_fusion), kind=kCustom, calls=%fused_computation.1 | custom fusion | bytes 2688 | tf_op jit(solution)/shard_map/gather | solution.py:689
  12.4 0.0 copy-start.1
  12.4 0.0 copy-start.2
  12.4 0.0 copy-start.3
  12.5 0.0 copy-start.4
  12.5 0.0 copy-start.5
  12.5 0.1 reshape.241
  12.6 0.1 copy.12.start_ref
  12.8 0.0 copy-done.6
  12.8 1.0 fusion.2
  13.8 0.1 pad_maximum_fusion.1.sine
  13.9 0.1 pad_maximum_fusion.cosine
  14.1 0.0 copy-done.1
  14.1 0.0 copy-done.2
  14.1 0.0 copy-done.3
  14.1 0.0 copy-done.4
  14.1 0.0 copy-done.5
  14.1 138.0 %shard_map.100 = (bf16[8,4,128,128]{3,2,1,0:T(8,128)(2,1)S(1)}, bf16[2,7,32,16,128]{4,3,2,1,0:T(8,128)(2,1)}) custom-call(s32[32,7]{1,0:T(8,128)S(1)} %fusion.4.table, bf16[128,5120]{1,0:T(8,128)(2,1)S(1)} %copy-done.1, f32[1,5120]{1,0:T(1,128)S(1)} %bitcast.17, bf16[80,1024]{1,0:T(8,128)(2,1)S(1)} %copy-done.2, bf16[5120,128]{1,0:T(8,128)(2,1)} %wk.1, ...), custom_call_target="tpu_custom_call" | custom-call | flops 6710886400 | bytes 10485760 | tf_op jit(solution)/shard_map/pallas_call | solution.py:582
  152.1 0.0 copy-start
  152.1 1.5 copy-done
  153.6 23.9 %shard_map.101 = bf16[512,1024]{1,0:T(8,128)(2,1)} custom-call(s32[512,1]{1,0:T(8,128)S(1)} %copy.12.start_ref, bf16[8,512,128]{2,1,0:T(8,128)(2,1)S(1)} %bitcast.16, bf16[2,7,512,128]{3,2,1,0:T(8,128)(2,1)S(1)} %bitcast.15), custom_call_target="tpu_custom_call" | custom-call | tf_op jit(solution)/shard_map/pallas_call | solution.py:646
  (9 shorter events, 0.1 us)
Async XLA Ops:
  10.5 2.2 %copy-start.6 = (f32[64]{0:T(128)S(1)}, f32[64]{0:T(128)}, u32[]{:S(2)}) copy-start(f32[64]{0:T(128)} %constant.162.clone) | copy-start | bytes 772
  12.4 1.7 copy-start.1
  12.4 1.7 copy-start.2
  12.4 1.7 copy-start.3
  12.5 1.6 copy-start.4
  12.5 1.6 copy-start.5
  152.1 1.5 copy-start

commit v4 on v3

--- a/solution.py
+++ b/solution.py
@@ -186,23 +186,10 @@
         left.start()
         core(s, ref).start()
 
-    def in_order(upper, lower):
-        def step(t, carry):
-            i = t - d
-
-            @pl.when((i >= 0) & (i < 4))
-            def _():
-                upper(i)
-
-            j = t - 4 + d
-
-            @pl.when((j >= 0) & (j < 4))
-            def _():
-                lower(j)
-
-            return carry
-
-        lax.fori_loop(0, 8, step, 0)
+    def when_four(i, act):
+        @pl.when((i >= 0) & (i < 4))
+        def _():
+            act(i)
 
     def z_upper(i):
         ref = slot(i, zh_u, y)
@@ -243,7 +230,89 @@
 
         spread(4 + i, ref)
 
-    in_order(z_upper, z_lower)
+    rows = wk.shape[0] // 8
+
+    def part(i):
+        return pl.ds(pl.multiple_of((k * 4 + i) * rows, 16), rows)
+
+    def key_part(i):
+        return wkv_all.at[part(i), pl.ds(0, 128)]
+
+    def value_part(i):
+        return wkv_all.at[part(i), pl.ds(128, 128)]
+
+    def kv_core(n, ref):
+        return remote(ref, ref, kc_s.at[n], kc_r.at[n], other)
+
+    def kp(i):
+        return remote(key_part(i), key_part(i), kp_s.at[i], kp_r.at[i], up)
+
+    def km(i):
+        return remote(value_part(i), value_part(i), km_s.at[i], km_r.at[i], down)
+
+    y_l, y_r, y_far = (y + 3) % 4, (y + 1) % 4, (y + 2) % 4
+
+    def ring(i, s, zhalf):
+        ref = slot(i, zhalf, y_l)
+        y_own(s, ref)[0].wait_recv()
+
+        @pl.when(i % 2 == 0)
+        def _():
+            fwd_right(s // 2, ref).start()
+
+        core(8 + s, ref).start()
+        ref2 = slot(i, zhalf, y_r)
+        y_own(s, ref2)[1].wait_recv()
+
+        @pl.when(i % 2 == 1)
+        def _():
+            fwd_left(s // 2, ref2).start()
+
+        core(16 + s, ref2).start()
+
+    def kv_upper(i):
+        @pl.when(d != 0)
+        def _():
+            kp(i).wait_recv()
+            kv_core(i, key_part(i)).start()
+
+            @pl.when(d != 3)
+            def _():
+                kp(i).start()
+
+    def kv_lower(i):
+        @pl.when(d != 0)
+        def _():
+            km(i).wait_recv()
+            kv_core(4 + i, value_part(i)).start()
+
+            @pl.when(d != 1)
+            def _():
+                km(i).start()
+
+    def ring_upper(i):
+        ring(i, i, zh_u)
+
+    def ring_lower(i):
+        ring(i, 4 + i, zh_d)
+
+    def step(t, carry):
+        when_four(t - d, z_upper)
+        when_four(t - 4 + d, z_lower)
+
+        @pl.when((d == 0) & (t == 3))
+        def _():
+            for i in range(4):
+                kp(i).start()
+                km(i).start()
+
+        when_four(t - 4 - d, kv_upper)
+        when_four(t - 8 + d, kv_lower)
+        when_four(t - 4 - d, ring_upper)
+        when_four(t - 8 + d, ring_lower)
+        return carry
+
+    lax.fori_loop(0, 7, step, 0)
 
     left_x, right_x, far_x = (x + 3) % 4, (x + 1) % 4, (x + 2) % 4
     tok_copy(0, left_x, 0, x_dev[1]).wait_recv()
@@ -253,76 +322,7 @@
     fwd_b = tok_copy(5, right_x, 1, x_dev[3])
     fwd_b.start()
 
-    rows = wk.shape[0] // 8
-
-    def part(i):
-        return pl.ds(pl.multiple_of((k * 4 + i) * rows, 16), rows)
-
-    def key_part(i):
-        return wkv_all.at[part(i), pl.ds(0, 128)]
-
-    def value_part(i):
-        return wkv_all.at[part(i), pl.ds(128, 128)]
-
-    def kv_core(n, ref):
-        return remote(ref, ref, kc_s.at[n], kc_r.at[n], other)
-
-    def kp(i):
-        return remote(key_part(i), key_part(i), kp_s.at[i], kp_r.at[i], up)
-
-    def km(i):
-        return remote(value_part(i), value_part(i), km_s.at[i], km_r.at[i], down)
-
-    y_l, y_r, y_far = (y + 3) % 4, (y + 1) % 4, (y + 2) % 4
-
-    def ring(i, s, zhalf):
-        ref = slot(i, zhalf, y_l)
-        y_own(s, ref)[0].wait_recv()
-
-        @pl.when(i % 2 == 0)
-        def _():
-            fwd_right(s // 2, ref).start()
-
-        core(8 + s, ref).start()
-        ref2 = slot(i, zhalf, y_r)
-        y_own(s, ref2)[1].wait_recv()
-
-        @pl.when(i % 2 == 1)
-        def _():
-            fwd_left(s // 2, ref2).start()
-
-        core(16 + s, ref2).start()
-
-    def kv_upper(i):
-        @pl.when(d == 0)
-        def _():
-            kp(i).start()
-            km(i).start()
-
-        @pl.when(d != 0)
-        def _():
-            kp(i).wait_recv()
-            kv_core(i, key_part(i)).start()
-
-        @pl.when((d == 1) | (d == 2))
-        def _():
-            kp(i).start()
-
-        ring(i, i, zh_u)
-
-    def kv_lower(i):
-        @pl.when(d != 0)
-        def _():
-            km(i).wait_recv()
-            kv_core(4 + i, value_part(i)).start()
-
-        @pl.when(d >= 2)
-        def _():
-            km(i).start()
-
-        ring(i, 4 + i, zh_d)
-
-    in_order(kv_upper, kv_lower)
+    lax.fori_loop(7, 12, step, 0)
 
     tok_copy(1, left_x, 1, x_dev[1]).wait_recv()
     tok_copy(2, right_x, 0, x_dev[3]).wait_recv()
@@ -395,7 +395,12 @@
 
         core(24 + s, ref).start()
 
-    in_order(far_upper, far_lower)
+    def far_step(t, carry):
+        when_four(t - d, far_upper)
+        when_four(t - 4 + d, far_lower)
+        return carry
+
+    lax.fori_loop(0, 8, far_step, 0)
 
     any_w = w_slot(me)
 
@@ -607,54 +612,73 @@
     )(table, tokens, norm_gain, w_query, w_key, w_value, q_gain, k_gain, cosine, sine)
 
 
-def attend_kernel(start_ref, q_ref, kv_ref, o_ref):
-    _, length, head_size = q_ref.shape
+def attend_kernel(q_doc, k_doc, q_ref, kv_ref, o_ref, keys, values, q_mask):
+    heads, length, size = q_ref.shape
+    span = 6 * length
     step = 256
-    scale = head_size ** (-0.5) * math.log2(math.e)
-    for r in range(length // step):
+    scale = size ** (-0.5) * math.log2(math.e)
+    lane = lax.broadcasted_iota(jnp.int32, (length, 128), 1)
+    q_mask[...] = jnp.where(q_doc[...] == lane, 0.0, -1e30).astype(BF16)
+    for i in range(7):
+        rows = pl.ds(i * length, length)
+        keys[rows, :128] = kv_ref[0, i]
+        keys[rows, 128:] = jnp.where(k_doc[rows, :] == lane, 1.0, 0.0).astype(BF16)
+        values[rows, :128] = kv_ref[1, i]
+        values[rows, 128:] = jnp.ones((length, 128), BF16)
+
+    def score(h, r):
         rows = pl.ds(r * step, step)
-        q = q_ref[0, rows, :]
-        start = start_ref[rows, :]
+        q = jnp.concatenate([q_ref[h, rows, :], q_mask[rows, :]], -1)
+        parts = [(r * step + at, length) for at in range(0, span, length)]
+        parts.append((r * step + span, step))
         tiles = []
         top = None
-        for i in range(7):
-            scores = lax.dot_general(
-                q, kv_ref[0, i], (((1,), (1,)), ((), ())), preferred_element_type=F32
+        for at, width in parts:
+            s = lax.dot_general(
+                q, keys[pl.ds(at, width), :], (((1,), (1,)), ((), ())), preferred_element_type=F32
             )
-            at = lax.broadcasted_iota(jnp.int32, scores.shape, 1) + (i - 6) * length
-            allowed = at >= start
-            if i == 6:
-                here = lax.broadcasted_iota(jnp.int32, scores.shape, 0) + r * step
-                allowed = allowed & (at <= here)
-            scores = jnp.where(allowed, scores, -1e30)
-            tiles.append(scores)
-            best = jnp.max(scores, -1, keepdims=True)
-            top = best if top is None else jnp.maximum(top, best)
-        total = None
+            if width == step:
+                here = lax.broadcasted_iota(jnp.int32, s.shape, 0)
+                s = jnp.where(lax.broadcasted_iota(jnp.int32, s.shape, 1) <= here, s, -1e30)
+            tiles.append(s)
+            for c in range(0, width, 128):
+                best = s[:, c : c + 128]
+                top = best if top is None else jnp.maximum(top, best)
+        return parts, tiles, jnp.max(top, -1, keepdims=True)
+
+    def finish(h, r, parts, tiles, top):
         summed = None
-        for i in range(7):
-            weights = jnp.exp2((tiles[i] - top) * scale)
-            added = jnp.sum(weights, -1, keepdims=True)
-            part = jnp.dot(weights.astype(BF16), kv_ref[1, i], preferred_element_type=F32)
-            total = added if total is None else total + added
+        for (at, width), s in zip(parts, tiles):
+            e = jnp.exp2((s - top) * scale).astype(BF16)
+            part = jnp.dot(e, values[pl.ds(at, width), :], preferred_element_type=F32)
             summed = part if summed is None else summed + part
-        o_ref[rows, :] = (summed / total).astype(BF16)
-
-
-def attend(start, q, kv):
+        out = summed[:, :128] / summed[:, 128:]
+        o_ref[pl.ds(r * step, step), h * 128 : h * 128 + 128] = out.astype(BF16)
+
+    ahead = None
+    for h in range(heads):
+        for r in range(length // step):
+            now = (h, r) + score(h, r)
+            if ahead is not None:
+                finish(*ahead)
+            ahead = now
+    finish(*ahead)
+
+
+def attend(q_doc, k_doc, q, kv):
     heads, length, size = q.shape
     return pl.pallas_call(
         attend_kernel,
-        grid=(heads,),
         out_shape=jax.ShapeDtypeStruct((length, heads * size), BF16),
-        in_specs=[
-            pl.BlockSpec((length, 1), lambda h: (0, 0)),
-            pl.BlockSpec((1, length, size), lambda h: (h, 0, 0)),
-            pl.BlockSpec(kv.shape, lambda h: (0, 0, 0, 0)),
+        in_specs=[pl.BlockSpec(memory_space=pltpu.VMEM)] * 4,
+        out_specs=pl.BlockSpec(memory_space=pltpu.VMEM),
+        scratch_shapes=[
+            pltpu.VMEM((7 * length, 256), BF16),
+            pltpu.VMEM((7 * length, 256), BF16),
+            pltpu.VMEM((length, 128), BF16),
         ],
-        out_specs=pl.BlockSpec((length, size), lambda h: (0, h)),
-        compiler_params=pltpu.CompilerParams(vmem_limit_bytes=48 << 20),
-    )(start, q, kv)
+        compiler_params=pltpu.CompilerParams(vmem_limit_bytes=50 << 20),
+    )(q_doc, k_doc, q, kv)
 
 
 def shards(tokens, norm_gain, w_query, w_key, w_value, query_gain, key_gain, segments, block_of):
@@ -694,8 +718,9 @@
         query_gain[None, :], key_gain[None, :], cosine, sine,
     )
     first = block_of[x * 16 + rest] * length
-    start = (start_of(first, length) - first)[:, None]
-    return attend(start, q_mine.reshape(8, length, 128), kv.reshape(2, 7, length, 128))
+    padded = jnp.concatenate([jnp.full((6 * length,), 63, jnp.int32), segments])
+    k_doc = lax.dynamic_slice_in_dim(padded, first, 7 * length, 0)[:, None]
+    return attend(k_doc[6 * length :], k_doc, q_mine.reshape(8, length, 128), kv.reshape(2, 7, length, 128))
 
 
 def solution(mesh):

time: 178 us -> 169 us (0.949)
  the two profiles are of different devices: /device:TPU:7 before, /device:TPU:41 now
where the time goes in v4:
time: 169 us
  Pallas kernels  155 us (92%)
  local copies, waits for them, and re-layouts  7.34 us (4%)
  other arithmetic  3.92 us (2%)
  between operations  3.41 us (2%)
    pallas_call x1, Pallas kernels, front(): pl.pallas_call(front_kernel, out_shape=(jax.ShapeDtypeStruct((8, 4, rows,...  135 us
    pallas_call x1, Pallas kernels, attend(): pl.pallas_call(attend_kernel, out_shape=jax.ShapeDtypeStruct((length, hea...  19.3 us

profile of v4, /device:TPU:41, one launch (start us, length us, event | category | flops | bytes accessed | tf_op | source)
XLA Modules:
  0.0 169.2 jit_solution(5568896049222641838)
XLA Ops:
  0.0 1.5 fusion.17
  4.7 0.8 fusion.16
  5.6 0.8 select_reduce_fusion
  6.3 1.6 convert_reduce_fusion
  7.9 0.1 select_reduce_fusion.4
  8.1 0.8 pad_dynamic-slice_fusion
  8.9 1.4 gather_fusion
  10.2 0.1 add_maximum_fusion
  10.3 0.1 reshape.233
  10.4 0.0 copy-start.5
  10.4 0.0 copy-start.6
  10.5 1.9 %gather_fusion.1 = s32[224]{0:T(256)S(1)} fusion(s32[64]{0:T(128)S(1)} %select_reduce_fusion, s32[1024]{0:T(1024)S(1)} %pad_clamp_fusion), kind=kCustom, calls=%fused_computation.1 | custom fusion | bytes 2688 | tf_op jit(solution)/shard_map/gather | solution.py:713
  12.3 0.1 reshape.232
  12.5 0.0 copy-done.5
  12.5 0.1 pad_dynamic-slice_fusion.1
  12.6 0.1 copy.13.q_doc
  12.7 0.0 copy-done.6
  12.7 0.0 copy-start
  12.7 0.0 copy-start.1
  12.8 0.0 copy-start.2
  12.8 0.0 copy-start.3
  12.8 0.0 copy-start.4
  12.8 1.0 fusion.2
  13.8 0.1 pad_maximum_fusion.1.sine
  13.9 0.1 pad_maximum_fusion.cosine
  14.1 0.5 broadcast_in_dim.80.k_doc
  14.6 0.0 copy-done
  14.6 0.0 copy-done.1
  14.6 0.0 copy-done.2
  14.6 0.0 copy-done.3
  14.7 135.2 %shard_map.100 = (bf16[8,4,128,128]{3,2,1,0:T(8,128)(2,1)S(1)}, bf16[2,7,32,16,128]{4,3,2,1,0:T(8,128)(2,1)}) custom-call(s32[32,7]{1,0:T(8,128)S(1)} %fusion.4.table, bf16[128,5120]{1,0:T(8,128)(2,1)S(1)} %copy-done, f32[1,5120]{1,0:T(1,128)S(1)} %bitcast.16, bf16[80,1024]{1,0:T(8,128)(2,1)S(1)} %copy-done.1, bf16[5120,128]{1,0:T(8,128)(2,1)} %wk.1, ...), custom_call_target="tpu_custom_call" | custom-call | flops 6710886400 | bytes 10485760 | tf_op jit(solution)/shard_map/pallas_call | solution.py:587
  149.9 19.3 %shard_map.101 = bf16[512,1024]{1,0:T(8,128)(2,1)} custom-call(s32[512,1]{1,0:T(8,128)S(1)} %copy.13.q_doc, s32[3584,1]{1,0:T(8,128)S(1)} %broadcast_in_dim.80.k_doc, bf16[8,512,128]{2,1,0:T(8,128)(2,1)S(1)} %bitcast.15, bf16[2,7,512,128]{3,2,1,0:T(8,128)(2,1)} %bitcast.19), custom_call_target="tpu_custom_call" | custom-call | tf_op jit(solution)/shard_map/pallas_call | solution.py:670
  (9 shorter events, 0.1 us)
Async XLA Ops:
  10.4 2.0 %copy-start.5 = (s32[32768]{0:T(1024)S(1)}, s32[32768]{0:T(1024)}, u32[]{:S(2)}) copy-start(s32[32768]{0:T(1024)} %param.17) | copy-start | bytes 393220
  10.4 2.3 %copy-start.6 = (f32[64]{0:T(128)S(1)}, f32[64]{0:T(128)}, u32[]{:S(2)}) copy-start(f32[64]{0:T(128)} %constant.166.clone) | copy-start | bytes 772
  12.7 1.9 %copy-start = (bf16[128,5120]{1,0:T(8,128)(2,1)S(1)}, bf16[128,5120]{1,0:T(8,128)(2,1)}, u32[]{:S(2)}) copy-start(bf16[128,5120]{1,0:T(8,128)(2,1)} %tok.1) | copy-start | bytes 3932164
  12.7 1.9 %copy-start.1 = (bf16[80,1024]{1,0:T(8,128)(2,1)S(1)}, bf16[80,1024]{1,0:T(8,128)(2,1)}, u32[]{:S(2)}) copy-start(bf16[80,1024]{1,0:T(8,128)(2,1)} %wq.1) | copy-start | bytes 491524
  12.8 1.9 %copy-start.2 = (f32[5120]{0:T(1024)S(1)}, f32[5120]{0:T(1024)}, u32[]{:S(2)}) copy-start(f32[5120]{0:T(1024)} %param.11) | copy-start | bytes 61444
  12.8 1.9 %copy-start.3 = (f32[128]{0:T(128)S(1)}, f32[128]{0:T(128)}, u32[]{:S(2)}) copy-start(f32[128]{0:T(128)} %param.15) | copy-start | bytes 1540
  12.8 1.9 %copy-start.4 = (f32[128]{0:T(128)S(1)}, f32[128]{0:T(128)}, u32[]{:S(2)}) copy-start(f32[128]{0:T(128)} %param.16) | copy-start | bytes 1540

commit v5 on v4

--- a/solution.py
+++ b/solution.py
@@ -10,6 +10,7 @@
 MESH = pl.DeviceIdType.MESH
 BF16 = jnp.bfloat16
 F32 = jnp.float32
+ROPE_SCALE = 0.1 * math.log(4.0) + 1.0
 STEPS = (
     (1, 0), (0, 1), (3, 0), (0, 3), (1, 1), (3, 3), (1, 3), (3, 1),
     (2, 0), (0, 2), (2, 1), (1, 2), (2, 3), (3, 2), (2, 2),
@@ -43,10 +44,64 @@
     return c // 16, (c // 4) % 4, (c // 2) % 2, c % 2, lax.axis_index("tensor")
 
 
+def attend(q_ref, kv_ref, k_mask, q_mask, o_ref):
+    heads = q_ref.shape[0]
+    length = q_mask.shape[0]
+    span = 6 * length
+    step = 256
+    scale = 128 ** (-0.5) * math.log2(math.e)
+    ones = jnp.ones((step, 128), BF16)
+
+    def score(h, r):
+        quarters = step // 128
+        q = q_ref[h, pl.ds(r * quarters, quarters)].reshape(step, 128)
+        q = jnp.concatenate([q, q_mask[pl.ds(r * step, step), :]], -1)
+        tiles = []
+        top = None
+        for at in range(r * step, span + r * step + step, step):
+            rows = (at // length, pl.ds(at % length, step))
+            keys = jnp.concatenate([kv_ref[(0,) + rows], k_mask[rows]], -1)
+            s = lax.dot_general(q, keys, (((1,), (1,)), ((), ())), preferred_element_type=F32)
+            if at == span + r * step:
+                here = lax.broadcasted_iota(jnp.int32, s.shape, 0)
+                s = jnp.where(lax.broadcasted_iota(jnp.int32, s.shape, 1) <= here, s, -1e30)
+            tiles.append((rows, s))
+            for c in range(0, step, 128):
+                best = s[:, c : c + 128]
+                top = best if top is None else jnp.maximum(top, best)
+        return tiles, jnp.max(top, -1, keepdims=True)
+
+    def finish(h, r, tiles, top):
+        summed = None
+        for rows, s in tiles:
+            e = jnp.exp2((s - top) * scale).astype(BF16)
+            values = jnp.concatenate([kv_ref[(1,) + rows], ones], -1)
+            part = jnp.dot(e, values, preferred_element_type=F32)
+            summed = part if summed is None else summed + part
+        out = summed[:, :128] / summed[:, 128:]
+        columns = pl.ds(pl.multiple_of(h * 128, 128), 128)
+        o_ref[pl.ds(r * step, step), columns] = out.astype(BF16)
+
+    def some(g, carry):
+        ahead = None
+        for n in range(4):
+            for r in range(length // step):
+                h = g * 4 + n
+                now = (h, r) + score(h, r)
+                if ahead is not None:
+                    finish(*ahead)
+                ahead = now
+        finish(*ahead)
+        return carry
+
+    lax.fori_loop(0, heads // 4, some, 0)
+
+
 def front_kernel(
-    table, tok, norm_gain, wq, wk, wv, q_gain, k_gain, cosine, sine,
-    q_out, kv_all,
+    block_of, slot_of, segs, freqs, tok, norm_gain, wq, wk, wv, q_gain, k_gain,
+    o_ref,
     tok_all, wq_all, wkv_all, q_send, qx, kv_send, got, picked,
+    q_out, kv_all, cosine, sine, k_mask, q_mask,
     loc, tok_s, tok_r, w1_s, w1_r, zp_s, zp_r, zm_s, zm_r,
     yr_s, yr_r, yl_s, yl_r, fr_s, fr_r, fl_s, fl_r, co_s, co_r,
     kp_s, kp_r, km_s, km_r, kc_s, kc_r,
@@ -296,6 +351,40 @@
     def ring_lower(i):
         ring(i, 4 + i, zh_d)
 
+    lane = lax.broadcasted_iota(jnp.int32, (128, 128), 1)
+
+    def doc_row(at, absent):
+        return jnp.where(at >= 0, segs[jnp.maximum(at, 0)], absent).astype(F32)
+
+    def down_rows(row):
+        return jnp.broadcast_to(row, (128, 128)).T
+
+    def rope_table(n):
+        row = block_of[n * 16 + rest] * 4 + zl
+        docs = down_rows(segs[row].astype(F32))
+
+        def count(j, total):
+            return total + jnp.where(doc_row(row - 24 + j, -1) < docs, 1.0, 0.0)
+
+        before = lax.fori_loop(0, 25, count, jnp.zeros((128, 128), F32))
+        here = lax.broadcasted_iota(jnp.int32, (128, 1), 0).astype(F32)
+        offset = 3072.0 + here - jnp.sum(before, -1, keepdims=True)
+        angle = offset * freqs[...]
+        rows = pl.ds(pl.multiple_of(n * 128, 128), 128)
+        cosine[rows, :] = jnp.cos(angle) * ROPE_SCALE
+        turned = jnp.sin(angle) * ROPE_SCALE
+        sine[rows, :] = jnp.where(lane < 64, -turned, turned)
+
+    def mask_rows(n):
+        for j in range(4):
+            docs = down_rows(doc_row(block_of[me] * 4 - 24 + n * 4 + j, 63))
+            same = docs == lane.astype(F32)
+            k_mask[n, pl.ds(j * 128, 128), :] = jnp.where(same, 1.0, 0.0).astype(BF16)
+
+            @pl.when(n == 6)
+            def _():
+                q_mask[pl.ds(j * 128, 128), :] = jnp.where(same, 0.0, -1e30).astype(BF16)
+
     def step(t, carry):
         when_four(t - d, z_upper)
         when_four(t - 4 + d, z_lower)
@@ -310,6 +399,12 @@
         when_four(t - 8 + d, kv_lower)
         when_four(t - 4 - d, ring_upper)
         when_four(t - 8 + d, ring_lower)
+        when_four(t, rope_table)
+
+        @pl.when((t >= 4) & (t < 11))
+        def _():
+            mask_rows(t - 4)
+
         return carry
 
     lax.fori_loop(0, 7, step, 0)
@@ -465,21 +560,24 @@
     def _():
         own_piece.wait()
 
+    own_keys = pl.ds(pl.multiple_of(mine * 16, 16), 16)
+
     def plane(n):
         return remote(
-            picked.at[n], kv_all.at[:, :, mine], p2_s.at[n], p2_r.at[mine], half_plane(n)
+            picked.at[n], kv_all.at[:, :, own_keys], p2_s.at[n], p2_r.at[mine], half_plane(n)
         )
 
     def pick(n):
+        block = block_of[half_plane(n)[0]]
         for i in range(7):
-            picked[n, :, i] = got[table[n, i]]
+            picked[n, :, i] = got[slot_of[jnp.maximum(block - 6 + i, 0)]]
 
     for dx, dy, dk in PLACES:
         n = ((x + dx) % 4) * 8 + ((y + dy) % 4) * 2 + (k + dk) % 2
         pick(n)
         plane(n).start()
     pick(mine)
-    own_plane = pltpu.make_async_copy(picked.at[mine], kv_all.at[:, :, mine], loc.at[2])
+    own_plane = pltpu.make_async_copy(picked.at[mine], kv_all.at[:, :, own_keys], loc.at[2])
     own_plane.start()
 
     def pass_on(n, carry):
@@ -494,13 +592,11 @@
 
     lax.fori_loop(0, 4, pass_on, 0)
 
-    def drain_q(n, carry):
+    def q_here(n, carry):
         pltpu.make_async_copy(
             q_send.at[heads(n), 0], q_out.at[heads(n), zl], loc.at[3 + n]
         ).wait()
         for o in (1, 2, 3):
-            x_step(n, o).wait_send()
-            z_step(n, q_send, (zl + o) % 4).wait_send()
             frm = (zl - o + 4) % 4
             remote(
                 q_send.at[heads(n), 0], q_out.at[heads(n), frm], qz_s.at[n, o], qz_r.at[n, o],
@@ -508,6 +604,26 @@
             ).wait_recv()
         return carry
 
+    lax.fori_loop(0, 4, q_here, 0)
+    own_plane.wait()
+
+    def plane_here(o, carry):
+        n = (mine + o) % 32
+        theirs = pl.ds(pl.multiple_of(n * 16, 16), 16)
+        remote(
+            picked.at[n], kv_all.at[:, :, theirs], p2_s.at[n], p2_r.at[n], half_plane(n)
+        ).wait_recv()
+        return carry
+
+    lax.fori_loop(1, 32, plane_here, 0)
+    attend(q_out, kv_all, k_mask, q_mask, o_ref)
+
+    def drain_q(n, carry):
+        for o in (1, 2, 3):
+            x_step(n, o).wait_send()
+            z_step(n, q_send, (zl + o) % 4).wait_send()
+        return carry
+
     lax.fori_loop(0, 4, drain_q, 0)
 
     def drain_piece(r, carry):
@@ -518,14 +634,9 @@
         return carry
 
     lax.fori_loop(0, 16, drain_piece, 0)
-    own_plane.wait()
 
     def drain_plane(o, carry):
-        n = (mine + o) % 32
-        plane(n).wait_send()
-        remote(
-            picked.at[n], kv_all.at[:, :, n], p2_s.at[n], p2_r.at[n], half_plane(n)
-        ).wait_recv()
+        plane((mine + o) % 32).wait_send()
         return carry
 
     lax.fori_loop(1, 32, drain_plane, 0)
@@ -576,9 +687,8 @@
         w1.wait_send()
 
 
-def front(table, tokens, norm_gain, w_query, w_key, w_value, q_gain, k_gain, cosine, sine):
+def front(block_of, slot_of, segs, freqs, tokens, norm_gain, w_query, w_key, w_value, q_gain, k_gain):
     vmem = pl.BlockSpec(memory_space=pltpu.VMEM)
-    hbm = pl.BlockSpec(memory_space=pl.ANY)
     dma = pltpu.SemaphoreType.DMA
     pair = lambda *n: [dma(n), dma(n)]
     rows, width = tokens.shape
@@ -586,12 +696,9 @@
     flops = 2 * 4 * rows * width * (columns + 256)
     return pl.pallas_call(
         front_kernel,
-        out_shape=(
-            jax.ShapeDtypeStruct((8, 4, rows, 128), BF16),
-            jax.ShapeDtypeStruct((2, 7, 32, 16, 128), BF16),
-        ),
-        in_specs=[pl.BlockSpec(memory_space=pltpu.SMEM)] + [vmem] * 9,
-        out_specs=(hbm, hbm),
+        out_shape=jax.ShapeDtypeStruct((4 * rows, columns), BF16),
+        in_specs=[pl.BlockSpec(memory_space=pltpu.SMEM)] * 2 + [vmem] * 9,
+        out_specs=vmem,
         scratch_shapes=[
             pltpu.VMEM((4 * rows, width), BF16),
             pltpu.VMEM((width, columns), BF16),
@@ -601,126 +708,32 @@
             pltpu.VMEM((8, 4, 2, 16, 128), BF16),
             pltpu.VMEM((64, 2, 16, 128), BF16),
             pltpu.VMEM((32, 2, 7, 16, 128), BF16),
+            pltpu.VMEM((8, 4, rows, 128), BF16),
+            pltpu.VMEM((2, 7, 4 * rows, 128), BF16),
+            pltpu.VMEM((4 * rows, 128), F32),
+            pltpu.VMEM((4 * rows, 128), F32),
+            pltpu.VMEM((7, 4 * rows, 128), BF16),
+            pltpu.VMEM((4 * rows, 128), BF16),
             dma((7,)),
         ] + pair(6) + [dma((1,)), dma((4,))] + pair(4) + pair(4) + pair(8) + pair(8)
         + pair(4) + pair(4) + pair(32) + pair(4) + pair(4) + pair(8)
         + pair(4, 4) + pair(4, 4) + pair(16) + pair(32),
         cost_estimate=pl.CostEstimate(flops=flops, bytes_accessed=10 << 20, transcendentals=0),
         compiler_params=pltpu.CompilerParams(
-            collective_id=0, has_side_effects=True, vmem_limit_bytes=50 << 20
+            collective_id=0, has_side_effects=True, vmem_limit_bytes=56 << 20
         ),
-    )(table, tokens, norm_gain, w_query, w_key, w_value, q_gain, k_gain, cosine, sine)
-
-
-def attend_kernel(q_doc, k_doc, q_ref, kv_ref, o_ref, keys, values, q_mask):
-    heads, length, size = q_ref.shape
-    span = 6 * length
-    step = 256
-    scale = size ** (-0.5) * math.log2(math.e)
-    lane = lax.broadcasted_iota(jnp.int32, (length, 128), 1)
-    q_mask[...] = jnp.where(q_doc[...] == lane, 0.0, -1e30).astype(BF16)
-    for i in range(7):
-        rows = pl.ds(i * length, length)
-        keys[rows, :128] = kv_ref[0, i]
-        keys[rows, 128:] = jnp.where(k_doc[rows, :] == lane, 1.0, 0.0).astype(BF16)
-        values[rows, :128] = kv_ref[1, i]
-        values[rows, 128:] = jnp.ones((length, 128), BF16)
-
-    def score(h, r):
-        rows = pl.ds(r * step, step)
-        q = jnp.concatenate([q_ref[h, rows, :], q_mask[rows, :]], -1)
-        parts = [(r * step + at, length) for at in range(0, span, length)]
-        parts.append((r * step + span, step))
-        tiles = []
-        top = None
-        for at, width in parts:
-            s = lax.dot_general(
-                q, keys[pl.ds(at, width), :], (((1,), (1,)), ((), ())), preferred_element_type=F32
-            )
-            if width == step:
-                here = lax.broadcasted_iota(jnp.int32, s.shape, 0)
-                s = jnp.where(lax.broadcasted_iota(jnp.int32, s.shape, 1) <= here, s, -1e30)
-            tiles.append(s)
-            for c in range(0, width, 128):
-                best = s[:, c : c + 128]
-                top = best if top is None else jnp.maximum(top, best)
-        return parts, tiles, jnp.max(top, -1, keepdims=True)
-
-    def finish(h, r, parts, tiles, top):
-        summed = None
-        for (at, width), s in zip(parts, tiles):
-            e = jnp.exp2((s - top) * scale).astype(BF16)
-            part = jnp.dot(e, values[pl.ds(at, width), :], preferred_element_type=F32)
-            summed = part if summed is None else summed + part
-        out = summed[:, :128] / summed[:, 128:]
-        o_ref[pl.ds(r * step, step), h * 128 : h * 128 + 128] = out.astype(BF16)
-
-    ahead = None
-    for h in range(heads):
-        for r in range(length // step):
-            now = (h, r) + score(h, r)
-            if ahead is not None:
-                finish(*ahead)
-            ahead = now
-    finish(*ahead)
-
-
-def attend(q_doc, k_doc, q, kv):
-    heads, length, size = q.shape
-    return pl.pallas_call(
-        attend_kernel,
-        out_shape=jax.ShapeDtypeStruct((length, heads * size), BF16),
-        in_specs=[pl.BlockSpec(memory_space=pltpu.VMEM)] * 4,
-        out_specs=pl.BlockSpec(memory_space=pltpu.VMEM),
-        scratch_shapes=[
-            pltpu.VMEM((7 * length, 256), BF16),
-            pltpu.VMEM((7 * length, 256), BF16),
-            pltpu.VMEM((length, 128), BF16),
-        ],
-        compiler_params=pltpu.CompilerParams(vmem_limit_bytes=50 << 20),
-    )(q_doc, k_doc, q, kv)
+    )(block_of, slot_of, segs, freqs, tokens, norm_gain, w_query, w_key, w_value, q_gain, k_gain)
 
 
 def shards(tokens, norm_gain, w_query, w_key, w_value, query_gain, key_gain, segments, block_of):
-    x, y, zh, k, zl = place()
-    rest = y * 4 + zh * 2 + k
-    quarter = tokens.shape[0]
-    length = quarter * 4
-
-    ids = jnp.arange(48, dtype=jnp.int32)
-    starts = jnp.sum((segments[None, :] < ids[:, None]).astype(jnp.int32), 1)
-
-    def start_of(at, size):
-        doc = lax.dynamic_slice_in_dim(segments, at, size, 0)
-        return jnp.sum(jnp.where(doc[:, None] == ids[None, :], starts[None, :], 0), 1)
-
-    offsets = []
-    for other in range(4):
-        at = block_of[other * 16 + rest] * length + zl * quarter
-        offsets.append(at + jnp.arange(quarter, dtype=jnp.int32) - start_of(at, quarter))
-    offsets = jnp.concatenate(offsets)
-
-    angles = offsets.astype(F32)[:, None] * jnp.asarray(yarn_frequencies(128), F32)[None, :]
-    scale = 0.1 * math.log(4.0) + 1.0
-    cosine, sine = jnp.cos(angles) * scale, jnp.sin(angles) * scale
-    cosine = jnp.concatenate([cosine, cosine], -1)
-    sine = jnp.concatenate([-sine, sine], -1)
-
     blocks = jnp.arange(64, dtype=jnp.int32)
-    holder = jnp.sum(jnp.where(block_of[None, :] == blocks[:, None], blocks[None, :], 0), 1)
-    d = jnp.arange(32, dtype=jnp.int32)
-    wanted = block_of[ctx_of(d // 8, (d // 2) % 4, zh, d % 2)][:, None] - 6 + jnp.arange(7)[None, :]
-    source = holder[jnp.maximum(wanted, 0)]
-    table = (source % 16) * 4 + source // 16
-
-    q_mine, kv = front(
-        table, tokens, norm_gain[None, :], w_query, w_key, w_value,
-        query_gain[None, :], key_gain[None, :], cosine, sine,
+    slot = (blocks % 16) * 4 + blocks // 16
+    slot_of = jnp.sum(jnp.where(block_of[None, :] == blocks[:, None], slot[None, :], 0), 1)
+    freqs = jnp.asarray(yarn_frequencies(128) * 2, F32)
+    return front(
+        block_of, slot_of, segments.reshape(-1, 1, 128), freqs[None, :], tokens,
+        norm_gain[None, :], w_query, w_key, w_value, query_gain[None, :], key_gain[None, :],
     )
-    first = block_of[x * 16 + rest] * length
-    padded = jnp.concatenate([jnp.full((6 * length,), 63, jnp.int32), segments])
-    k_doc = lax.dynamic_slice_in_dim(padded, first, 7 * length, 0)[:, None]
-    return attend(k_doc[6 * length :], k_doc, q_mine.reshape(8, length, 128), kv.reshape(2, 7, length, 128))
 
 
 def solution(mesh):

time: 169 us -> 157 us (0.929)
  local copies, waits for them, and re-layouts: 7.34 us -> 2.26 us
  between operations: 3.41 us -> 0.01 us
  other arithmetic: 3.92 us -> 1.29 us
  Pallas kernels: 155 us -> 153 us
    gather x3 -> x0, local copies, waits for them, and re-layouts: 3.31 us -> none  [the longest x2 1.96 us: shards(): source = holder[jnp.maximum(wanted, 0)]]
    dynamic_slice x3 -> x0, local copies, waits for them, and re-layouts: 2.43 us -> none  [the longest x1 1.52 us: shards(): at = block_of[other * 16 + rest] * length + zl * quarter]
    unnamed x14 -> x1, local copies, waits for them, and re-layouts: 0.04 us -> 2.26 us
    pallas_call x2 -> x1, Pallas kernels: 155 us -> 153 us  [front(): pl.pallas_call(front_kernel, out_shape=jax.ShapeDtypeStruct((4 * rows, co...]
where the time goes in v5:
time: 157 us
  Pallas kernels  153 us (97%)
  local copies, waits for them, and re-layouts  2.26 us (1%)
    pallas_call x1, Pallas kernels, front(): pl.pallas_call(front_kernel, out_shape=jax.ShapeDtypeStruct((4 * rows, co...  153 us

profile of v5, /device:TPU:41, one launch (start us, length us, event | category | flops | bytes accessed | tf_op | source)
XLA Modules:
  0.0 157.0 jit_solution(14644073936787332319)
XLA Ops:
  0.0 1.3 select_reduce_fusion.slot_of
  1.3 153.5 %shard_map.100 = bf16[512,1024]{1,0:T(8,128)(2,1)} custom-call(s32[64]{0:T(128)} %block_of.1, s32[64]{0:T(128)} %select_reduce_fusion.slot_of, s32[256,1,128]{2,1,0:T(1,128)} %bitcast.4, f32[1,128]{1,0:T(1,128)} %constant.38.freqs, bf16[128,5120]{1,0:T(8,128)(2,1)} %tok.1, f32[1,5120]{1,0:T(1,128)} %bitcast.5, bf16[80,1024]{1,0:T(8,128)(2,1)} %wq.1, ...), custom_call_target="tpu_custom_call" | custom-call | flops 6710886400 | bytes 10485760 | tf_op jit(solution)/shard_map/pallas_call | solution.py:697
  154.7 2.3 %copy.12 = bf16[512,1024]{1,0:T(8,128)(2,1)} copy(bf16[512,1024]{1,0:T(8,128)(2,1)} %shard_map.100) | data formatting | bytes 2097152
  (1 shorter events, 0.0 us)

commit v6 on v5

--- a/solution.py
+++ b/solution.py
@@ -100,12 +100,12 @@
 def front_kernel(
     block_of, slot_of, segs, freqs, tok, norm_gain, wq, wk, wv, q_gain, k_gain,
     o_ref,
-    tok_all, wq_all, wkv_all, q_send, qx, kv_send, got, picked,
+    tok_all, wq_all, wkv_all, q_send, qx, kv_send, got_k, got_v, picked,
     q_out, kv_all, cosine, sine, k_mask, q_mask,
     loc, tok_s, tok_r, w1_s, w1_r, zp_s, zp_r, zm_s, zm_r,
     yr_s, yr_r, yl_s, yl_r, fr_s, fr_r, fl_s, fl_r, co_s, co_r,
     kp_s, kp_r, km_s, km_r, kc_s, kc_r,
-    qx_s, qx_r, qz_s, qz_r, p1_s, p1_r, p2_s, p2_r,
+    qx_s, qx_r, qz_s, qz_r, p1_s, p1_r, p2_s, p2_r, own_s,
 ):
     x, y, zh, k, zl = place()
     me = ctx_of(x, y, zh, k)
@@ -162,7 +162,7 @@
         wide = tok[rows, :].astype(F32)
         mean = jnp.mean(wide * wide, -1, keepdims=True)
         wide = wide * lax.rsqrt(mean + 1e-06) * norm_gain[...]
-        tok_all[pl.ds(pl.multiple_of(x * quarter + n * 16, 16), 16), :] = wide.astype(BF16)
+        tok_all[rows, :] = wide.astype(BF16)
         return carry
 
     lax.fori_loop(0, quarter // 16, norm_rows, 0)
@@ -175,23 +175,23 @@
 
     half = quarter // 2
 
-    def tok_copy(n, slot, part, dev):
-        ref = tok_all.at[pl.ds(pl.multiple_of(slot * quarter + part * half, 16), half)]
-        return remote(ref, ref, tok_s.at[n], tok_r.at[n], dev)
+    def tok_copy(n, src, dst, part, dev):
+        ref = lambda slot: tok_all.at[pl.ds(slot * quarter + part * half, half)]
+        return remote(ref(src), ref(dst), tok_s.at[n], tok_r.at[n], dev)
 
     def w_slot(c):
         return wq_all.at[pl.ds(pl.multiple_of(c * w_rows, 16), w_rows)]
 
     w_rows = wq.shape[0]
     sends = [
-        tok_copy(0, x, 0, x_dev[1]),
-        tok_copy(3, x, 1, x_dev[3]),
-        tok_copy(1, x, 1, x_dev[1]),
-        tok_copy(2, x, 0, x_dev[3]),
+        tok_copy(0, 0, 2, 0, x_dev[1]),
+        tok_copy(3, 0, 1, 1, x_dev[3]),
+        tok_copy(1, 0, 2, 1, x_dev[1]),
+        tok_copy(2, 0, 1, 0, x_dev[3]),
     ]
     w1_index = (x - zl + 4) % 4
     w1 = remote(wq, w_slot(me), w1_s.at[0], w1_r.at[w1_index], (ctx_of(zl, y, zh, k), zl))
-    own_w = pltpu.make_async_copy(wq, w_slot(me), loc.at[1])
+    own_w = pltpu.make_async_copy(wq, w_slot(me), loc.at[2])
 
     @pl.when(d != 0)
     def _():
@@ -360,7 +360,7 @@
         return jnp.broadcast_to(row, (128, 128)).T
 
     def rope_table(n):
-        row = block_of[n * 16 + rest] * 4 + zl
+        row = block_of[((x + n + n // 2 - n // 3 * 2) % 4) * 16 + rest] * 4 + zl
         docs = down_rows(segs[row].astype(F32))
 
         def count(j, total):
@@ -409,20 +409,17 @@
 
     lax.fori_loop(0, 7, step, 0)
 
-    left_x, right_x, far_x = (x + 3) % 4, (x + 1) % 4, (x + 2) % 4
-    tok_copy(0, left_x, 0, x_dev[1]).wait_recv()
-    fwd_a = tok_copy(4, left_x, 0, x_dev[1])
+    tok_copy(0, 0, 2, 0, x_dev[1]).wait_recv()
+    fwd_a = tok_copy(4, 2, 3, 0, x_dev[1])
     fwd_a.start()
-    tok_copy(3, right_x, 1, x_dev[3]).wait_recv()
-    fwd_b = tok_copy(5, right_x, 1, x_dev[3])
+    tok_copy(3, 0, 1, 1, x_dev[3]).wait_recv()
+    fwd_b = tok_copy(5, 1, 3, 1, x_dev[3])
     fwd_b.start()
 
     lax.fori_loop(7, 12, step, 0)
 
-    tok_copy(1, left_x, 1, x_dev[1]).wait_recv()
-    tok_copy(2, right_x, 0, x_dev[3]).wait_recv()
-    tok_copy(4, far_x, 0, x_dev[1]).wait_recv()
-    tok_copy(5, far_x, 1, x_dev[3]).wait_recv()
+    tok_copy(1, 0, 2, 1, x_dev[1]).wait_recv()
+    tok_copy(2, 0, 1, 0, x_dev[3]).wait_recv()
 
     @pl.when(d != 0)
     def _():
@@ -433,43 +430,74 @@
 
         lax.fori_loop(0, 4, core_part, 0)
 
-    def turn(t, gain):
+    def turn(t, gain, rows):
         t = t * lax.rsqrt(jnp.mean(t * t, -1, keepdims=True) + 1e-06) * gain[...]
-        return (t * cosine[...] + pltpu.roll(t, 64, 1) * sine[...]).astype(BF16)
-
-    both = jnp.dot(tok_all[...], wkv_all[...], preferred_element_type=F32)
-    key = turn(both[:, :128], k_gain)
-    value = both[:, 128:].astype(BF16)
-    for p in range(8):
-        for n in range(4):
-            at = n * 128 + p * 16
-            kv_send[p, n, 0] = key[at : at + 16]
-            kv_send[p, n, 1] = value[at : at + 16]
-
-    def piece(r):
-        p = (r // 4) * 2 + r % 2
-        return remote(
-            kv_send.at[p], got.at[pl.ds(rest * 4, 4)], p1_s.at[r], p1_r.at[rest], (zl * 16 + r, x)
-        )
-
-    own_piece = pltpu.make_async_copy(
-        kv_send.at[(rest // 4) * 2 + rest % 2], got.at[pl.ds(rest * 4, 4)], loc.at[0]
-    )
-
-    def send_piece(o, carry):
-        r = (rest + o) % 16
-
-        @pl.when((x != zl) | (r != rest))
-        def _():
-            piece(r).start()
-
-        return carry
-
-    lax.fori_loop(0, 16, send_piece, 0)
-
-    @pl.when(x == zl)
-    def _():
-        own_piece.start()
+        return (t * cosine[rows, :] + pltpu.roll(t, 64, 1) * sine[rows, :]).astype(BF16)
+
+    def keys_values(first, count):
+        rows = pl.ds(first * quarter, count * quarter)
+        both = jnp.dot(tok_all[rows, :], wkv_all[...], preferred_element_type=F32)
+        key = turn(both[:, :128], k_gain, rows)
+        value = both[:, 128:].astype(BF16)
+        for p in range(8):
+            for n in range(count):
+                at = n * quarter + p * 16
+                kv_send[0, p, first + n] = key[at : at + 16]
+                kv_send[1, p, first + n] = value[at : at + 16]
+
+    early = pl.ds(0, 3)
+
+    def piece(m, r, src_rest, dst_p):
+        if m == 0:
+            src, dst = kv_send.at[0, dst_p, early], got_k.at[pl.ds(src_rest * 4, 3)]
+        elif m == 1:
+            src, dst = kv_send.at[0, dst_p, 3], got_k.at[src_rest * 4 + 3]
+        else:
+            src, dst = kv_send.at[1, dst_p], got_v.at[pl.ds(src_rest * 4, 4)]
+        return src, dst, p1_s.at[m, r], p1_r.at[m, src_rest]
+
+    def to_piece(r):
+        return (r // 4) * 2 + r % 2
+
+    def send_pieces(m):
+        def send_piece(o, carry):
+            r = (rest + o) % 16
+
+            @pl.when((x != zl) | (r != rest))
+            def _():
+                remote(*piece(m, r, rest, to_piece(r)), (zl * 16 + r, x)).start()
+
+            return carry
+
+        lax.fori_loop(0, 16, send_piece, 0)
+
+        @pl.when(x == zl)
+        def _():
+            src, dst, _, _ = piece(m, rest, rest, to_piece(rest))
+            pltpu.make_async_copy(src, dst, own_s.at[m]).start()
+
+    def wait_pieces(m):
+        def wait_piece(r, carry):
+            @pl.when((x != zl) | (r != rest))
+            def _():
+                remote(*piece(m, r, r, 0), (zl * 16 + r, x)).wait_recv()
+
+            return carry
+
+        lax.fori_loop(0, 16, wait_piece, 0)
+
+        @pl.when(x == zl)
+        def _():
+            src, dst, _, _ = piece(m, rest, rest, to_piece(rest))
+            pltpu.make_async_copy(src, dst, own_s.at[m]).wait()
+
+    keys_values(0, 3)
+    send_pieces(0)
+    tok_copy(4, 2, 3, 0, x_dev[1]).wait_recv()
+    tok_copy(5, 1, 3, 1, x_dev[3]).wait_recv()
+    keys_values(3, 1)
+    send_pieces(1)
+    send_pieces(2)
 
     def far_upper(i):
         finish(i, i, zh_u)
@@ -509,16 +537,15 @@
         return pl.ds(n * 2, 2)
 
     def x_step(n, o):
-        to = (x + o) % 4
         return remote(
-            q_send.at[heads(n), to], qx.at[heads(n), x], qx_s.at[n, o], qx_r.at[n, o],
-            (ctx_of(to, y, zh, k), zl),
+            q_send.at[heads(n), (0, 1, 3, 2)[o]], qx.at[heads(n), x], qx_s.at[n, o],
+            qx_r.at[n, o], x_dev[o],
         )
 
     def z_step(n, src, to):
         o = (to - zl + 4) % 4
         return remote(
-            src.at[heads(n), to], q_out.at[heads(n), zl], qz_s.at[n, o], qz_r.at[n, o], (me, to)
+            src, q_out.at[heads(n), zl], qz_s.at[n, o], qz_r.at[n, o], (me, to)
         )
 
     def z_move(n, src, frm):
@@ -529,56 +556,49 @@
         @pl.when(frm == zl)
         def _():
             pltpu.make_async_copy(
-                src.at[heads(n), frm], q_out.at[heads(n), zl], loc.at[3 + n]
+                src, q_out.at[heads(n), zl], loc.at[3 + n]
             ).start()
 
     def project(n, carry):
         columns = pl.ds(pl.multiple_of(n * 256, 256), 256)
         both = jnp.dot(tok_all[...], wq_all[:, columns], preferred_element_type=F32)
         for h in range(2):
-            head = turn(both[:, h * 128 : h * 128 + 128], q_gain)
+            head = turn(both[:, h * 128 : h * 128 + 128], q_gain, pl.ds(0, 4 * quarter))
             q_send[n * 2 + h] = head.reshape(4, quarter, 128)
         for o in (1, 3, 2):
             x_step(n, o).start()
-        z_move(n, q_send, x)
+        z_move(n, q_send.at[heads(n), 0], x)
         return carry
 
     lax.fori_loop(0, 4, project, 0)
 
-    def wait_piece(r, carry):
-        @pl.when((x != zl) | (r != rest))
-        def _():
-            remote(
-                kv_send.at[0], got.at[pl.ds(r * 4, 4)], p1_s.at[0], p1_r.at[r], (zl * 16 + r, x)
-            ).wait_recv()
-
-        return carry
-
-    lax.fori_loop(0, 16, wait_piece, 0)
-
-    @pl.when(x == zl)
-    def _():
-        own_piece.wait()
-
     own_keys = pl.ds(pl.multiple_of(mine * 16, 16), 16)
 
-    def plane(n):
+    def plane(m, n):
         return remote(
-            picked.at[n], kv_all.at[:, :, own_keys], p2_s.at[n], p2_r.at[mine], half_plane(n)
+            picked.at[m, n], kv_all.at[m, :, own_keys], p2_s.at[m, n], p2_r.at[m, mine],
+            half_plane(n),
         )
 
-    def pick(n):
+    def pick(m, n):
         block = block_of[half_plane(n)[0]]
         for i in range(7):
-            picked[n, :, i] = got[slot_of[jnp.maximum(block - 6 + i, 0)]]
-
-    for dx, dy, dk in PLACES:
-        n = ((x + dx) % 4) * 8 + ((y + dy) % 4) * 2 + (k + dk) % 2
-        pick(n)
-        plane(n).start()
-    pick(mine)
-    own_plane = pltpu.make_async_copy(picked.at[mine], kv_all.at[:, :, own_keys], loc.at[2])
-    own_plane.start()
+            slot = slot_of[jnp.maximum(block - 6 + i, 0)]
+            picked[m, n, i] = (got_k, got_v)[m][slot]
+
+    def send_plane(m):
+        for dx, dy, dk in PLACES:
+            n = ((x + dx) % 4) * 8 + ((y + dy) % 4) * 2 + (k + dk) % 2
+            pick(m, n)
+            plane(m, n).start()
+        pick(m, mine)
+        pltpu.make_async_copy(picked.at[m, mine], kv_all.at[m, :, own_keys], loc.at[m]).start()
+
+    wait_pieces(0)
+    wait_pieces(1)
+    send_plane(0)
+    wait_pieces(2)
+    send_plane(1)
 
     def pass_on(n, carry):
         for o in (1, 3, 2):
@@ -587,7 +607,7 @@
                 q_send.at[heads(n), 0], qx.at[heads(n), frm], qx_s.at[n, o], qx_r.at[n, o],
                 (ctx_of(frm, y, zh, k), zl),
             ).wait_recv()
-            z_move(n, qx, frm)
+            z_move(n, qx.at[heads(n), frm], frm)
         return carry
 
     lax.fori_loop(0, 4, pass_on, 0)
@@ -605,14 +625,17 @@
         return carry
 
     lax.fori_loop(0, 4, q_here, 0)
-    own_plane.wait()
+    for m in range(2):
+        pltpu.make_async_copy(picked.at[m, mine], kv_all.at[m, :, own_keys], loc.at[m]).wait()
 
     def plane_here(o, carry):
         n = (mine + o) % 32
         theirs = pl.ds(pl.multiple_of(n * 16, 16), 16)
-        remote(
-            picked.at[n], kv_all.at[:, :, theirs], p2_s.at[n], p2_r.at[n], half_plane(n)
-        ).wait_recv()
+        for m in range(2):
+            remote(
+                picked.at[m, n], kv_all.at[m, :, theirs], p2_s.at[m, n], p2_r.at[m, n],
+                half_plane(n),
+            ).wait_recv()
         return carry
 
     lax.fori_loop(1, 32, plane_here, 0)
@@ -621,7 +644,7 @@
     def drain_q(n, carry):
         for o in (1, 2, 3):
             x_step(n, o).wait_send()
-            z_step(n, q_send, (zl + o) % 4).wait_send()
+            z_step(n, q_send.at[heads(n), 0], (zl + o) % 4).wait_send()
         return carry
 
     lax.fori_loop(0, 4, drain_q, 0)
@@ -629,14 +652,16 @@
     def drain_piece(r, carry):
         @pl.when((x != zl) | (r != rest))
         def _():
-            piece(r).wait_send()
+            for m in range(3):
+                remote(*piece(m, r, rest, to_piece(r)), (zl * 16 + r, x)).wait_send()
 
         return carry
 
     lax.fori_loop(0, 16, drain_piece, 0)
 
     def drain_plane(o, carry):
-        plane((mine + o) % 32).wait_send()
+        for m in range(2):
+            plane(m, (mine + o) % 32).wait_send()
         return carry
 
     lax.fori_loop(1, 32, drain_plane, 0)
@@ -705,9 +730,10 @@
             pltpu.VMEM((width, 256), BF16),
             pltpu.VMEM((8, 4, rows, 128), BF16),
             pltpu.VMEM((8, 4, rows, 128), BF16),
-            pltpu.VMEM((8, 4, 2, 16, 128), BF16),
-            pltpu.VMEM((64, 2, 16, 128), BF16),
-            pltpu.VMEM((32, 2, 7, 16, 128), BF16),
+            pltpu.VMEM((2, 8, 4, 16, 128), BF16),
+            pltpu.VMEM((64, 16, 128), BF16),
+            pltpu.VMEM((64, 16, 128), BF16),
+            pltpu.VMEM((2, 32, 7, 16, 128), BF16),
             pltpu.VMEM((8, 4, rows, 128), BF16),
             pltpu.VMEM((2, 7, 4 * rows, 128), BF16),
             pltpu.VMEM((4 * rows, 128), F32),
@@ -717,7 +743,7 @@
             dma((7,)),
         ] + pair(6) + [dma((1,)), dma((4,))] + pair(4) + pair(4) + pair(8) + pair(8)
         + pair(4) + pair(4) + pair(32) + pair(4) + pair(4) + pair(8)
-        + pair(4, 4) + pair(4, 4) + pair(16) + pair(32),
+        + pair(4, 4) + pair(4, 4) + pair(3, 16) + pair(2, 32) + [dma((3,))],
         cost_estimate=pl.CostEstimate(flops=flops, bytes_accessed=10 << 20, transcendentals=0),
         compiler_params=pltpu.CompilerParams(
             collective_id=0, has_side_effects=True, vmem_limit_bytes=56 << 20
@@ -727,7 +753,8 @@
 
 def shards(tokens, norm_gain, w_query, w_key, w_value, query_gain, key_gain, segments, block_of):
     blocks = jnp.arange(64, dtype=jnp.int32)
-    slot = (blocks % 16) * 4 + blocks // 16
+    ahead = (blocks // 16 - lax.axis_index("tensor") + 4) % 4
+    slot = (blocks % 16) * 4 + ahead + ahead // 2 - ahead // 3 * 2
     slot_of = jnp.sum(jnp.where(block_of[None, :] == blocks[:, None], slot[None, :], 0), 1)
     freqs = jnp.asarray(yarn_frequencies(128) * 2, F32)
     return front(

time: 157 us -> 157 us (level)
  no operation moved by 1% of the time
where the time goes in v6:
time: 157 us; the launch traced here: 156 us
  Pallas kernels  152 us (97%)
  local copies, waits for them, and re-layouts  2.26 us (1%)
    pallas_call x1, Pallas kernels, front(): pl.pallas_call(front_kernel, out_shape=jax.ShapeDtypeStruct((4 * rows, co...  152 us

profile of v6, /device:TPU:41, one launch (start us, length us, event | category | flops | bytes accessed | tf_op | source)
XLA Modules:
  0.0 155.9 jit_solution(17419024147493172338)
XLA Ops:
  0.0 1.3 select_reduce_fusion.slot_of
  1.3 152.3 %shard_map.100 = bf16[512,1024]{1,0:T(8,128)(2,1)} custom-call(s32[64]{0:T(128)} %block_of.1, s32[64]{0:T(128)} %select_reduce_fusion.slot_of, s32[256,1,128]{2,1,0:T(1,128)} %bitcast.4, f32[1,128]{1,0:T(1,128)} %constant.68.freqs, bf16[128,5120]{1,0:T(8,128)(2,1)} %tok.1, f32[1,5120]{1,0:T(1,128)} %bitcast.5, bf16[80,1024]{1,0:T(8,128)(2,1)} %wq.1, ...), custom_call_target="tpu_custom_call" | custom-call | flops 6710886400 | bytes 10485760 | tf_op jit(solution)/shard_map/pallas_call | solution.py:722
  153.6 2.3 %copy.12 = bf16[512,1024]{1,0:T(8,128)(2,1)} copy(bf16[512,1024]{1,0:T(8,128)(2,1)} %shard_map.100) | data formatting | bytes 2097152
  (1 shorter events, 0.0 us)

commit v7 on v6

--- a/solution.py
+++ b/solution.py
@@ -165,7 +165,6 @@
         tok_all[rows, :] = wide.astype(BF16)
         return carry
 
-    lax.fori_loop(0, quarter // 16, norm_rows, 0)
     pl.semaphore_wait(barrier, 8 + 3 + 15 + 31 + ((x - zl + 4) % 4 + 3) // 4)
 
     def remote(src, dst, ss, rs, dev):
@@ -201,13 +200,13 @@
     def _():
         own_w.start()
 
-    for copy in sends:
-        copy.start()
+    own_k = pltpu.make_async_copy(wk, wkv_all.at[:, pl.ds(0, 128)], loc.at[0])
+    own_v = pltpu.make_async_copy(wv, wkv_all.at[:, pl.ds(128, 128)], loc.at[1])
 
     @pl.when(d == 0)
     def _():
-        wkv_all[:, :128] = wk[...]
-        wkv_all[:, 128:] = wv[...]
+        own_k.start()
+        own_v.start()
 
     def slot(i, zhalf, yy):
         return w_slot(ctx_of((x + i) % 4, yy, zhalf, k))
@@ -391,6 +390,8 @@
 
         @pl.when((d == 0) & (t == 3))
         def _():
+            own_k.wait()
+            own_v.wait()
             for i in range(4):
                 kp(i).start()
                 km(i).start()
@@ -399,7 +400,7 @@
         when_four(t - 8 + d, kv_lower)
         when_four(t - 4 - d, ring_upper)
         when_four(t - 8 + d, ring_lower)
-        when_four(t, rope_table)
+        when_four(t - 1, rope_table)
 
         @pl.when((t >= 4) & (t < 11))
         def _():
@@ -407,7 +408,11 @@
 
         return carry
 
-    lax.fori_loop(0, 7, step, 0)
+    lax.fori_loop(0, 1, step, 0)
+    lax.fori_loop(0, quarter // 16, norm_rows, 0)
+    for copy in sends:
+        copy.start()
+    lax.fori_loop(1, 7, step, 0)
 
     tok_copy(0, 0, 2, 0, x_dev[1]).wait_recv()
     fwd_a = tok_copy(4, 2, 3, 0, x_dev[1])
@@ -570,8 +575,6 @@
         z_move(n, q_send.at[heads(n), 0], x)
         return carry
 
-    lax.fori_loop(0, 4, project, 0)
-
     own_keys = pl.ds(pl.multiple_of(mine * 16, 16), 16)
 
     def plane(m, n):
@@ -593,12 +596,6 @@
             plane(m, n).start()
         pick(m, mine)
         pltpu.make_async_copy(picked.at[m, mine], kv_all.at[m, :, own_keys], loc.at[m]).start()
-
-    wait_pieces(0)
-    wait_pieces(1)
-    send_plane(0)
-    wait_pieces(2)
-    send_plane(1)
 
     def pass_on(n, carry):
         for o in (1, 3, 2):
@@ -610,7 +607,15 @@
             z_move(n, qx.at[heads(n), frm], frm)
         return carry
 
-    lax.fori_loop(0, 4, pass_on, 0)
+    lax.fori_loop(0, 4, project, 0)
+    lax.fori_loop(0, 2, pass_on, 0)
+    wait_pieces(0)
+    wait_pieces(1)
+    send_plane(0)
+    lax.fori_loop(2, 4, pass_on, 0)
+    wait_pieces(2)
+    send_plane(1)
+
 
     def q_here(n, carry):
         pltpu.make_async_copy(
@@ -722,7 +727,8 @@
     return pl.pallas_call(
         front_kernel,
         out_shape=jax.ShapeDtypeStruct((4 * rows, columns), BF16),
-        in_specs=[pl.BlockSpec(memory_space=pltpu.SMEM)] * 2 + [vmem] * 9,
+        in_specs=[pl.BlockSpec(memory_space=pltpu.SMEM)] * 2 + [vmem] * 5
+        + [pl.BlockSpec(memory_space=pl.ANY)] * 2 + [vmem] * 2,
         out_specs=vmem,
         scratch_shapes=[
             pltpu.VMEM((4 * rows, width), BF16),

time: 157 us -> 153 us (0.975)
  Pallas kernels: 152 us -> 148 us
    pallas_call x1, Pallas kernels: 152 us -> 148 us  [front(): pl.pallas_call(front_kernel, out_shape=jax.ShapeDtypeStruct((4 * rows, co...]
where the time goes in v7:
time: 153 us; the launch traced here: 152 us
  Pallas kernels  148 us (97%)
  local copies, waits for them, and re-layouts  2.26 us (1%)
    pallas_call x1, Pallas kernels, front(): pl.pallas_call(front_kernel, out_shape=jax.ShapeDtypeStruct((4 * rows, co...  148 us

profile of v7, /device:TPU:41, one launch (start us, length us, event | category | flops | bytes accessed | tf_op | source)
XLA Modules:
  0.0 152.0 jit_solution(16509447767215458)
XLA Ops:
  0.0 1.3 select_reduce_fusion.slot_of
  1.3 148.4 %shard_map.100 = bf16[512,1024]{1,0:T(8,128)(2,1)} custom-call(s32[64]{0:T(128)} %block_of.1, s32[64]{0:T(128)} %select_reduce_fusion.slot_of, s32[256,1,128]{2,1,0:T(1,128)} %bitcast.4, f32[1,128]{1,0:T(1,128)} %constant.68.freqs, bf16[128,5120]{1,0:T(8,128)(2,1)} %tok.1, f32[1,5120]{1,0:T(1,128)} %bitcast.5, bf16[80,1024]{1,0:T(8,128)(2,1)} %wq.1, ...), custom_call_target="tpu_custom_call" | custom-call | flops 6710886400 | bytes 10485760 | tf_op jit(solution)/shard_map/pallas_call | solution.py:727
  149.7 2.3 %copy.12 = bf16[512,1024]{1,0:T(8,128)(2,1)} copy(bf16[512,1024]{1,0:T(8,128)(2,1)} %shard_map.100) | data formatting | bytes 2097152
  (1 shorter events, 0.0 us)

commit v8 on v7

--- a/solution.py
+++ b/solution.py
@@ -608,11 +608,10 @@
         return carry
 
     lax.fori_loop(0, 4, project, 0)
-    lax.fori_loop(0, 2, pass_on, 0)
+    lax.fori_loop(0, 4, pass_on, 0)
     wait_pieces(0)
     wait_pieces(1)
     send_plane(0)
-    lax.fori_loop(2, 4, pass_on, 0)
     wait_pieces(2)
     send_plane(1)
 

time: 153 us -> 155 us (1.013)
  Pallas kernels: 148 us -> 150 us
where the time goes in v8:
time: 155 us; the launch traced here: 153 us
  Pallas kernels  150 us (97%)
  local copies, waits for them, and re-layouts  2.26 us (1%)
    pallas_call x1, Pallas kernels, front(): pl.pallas_call(front_kernel, out_shape=jax.ShapeDtypeStruct((4 * rows, co...  150 us

profile of v8, /device:TPU:41, one launch (start us, length us, event | category | flops | bytes accessed | tf_op | source)
XLA Modules:
  0.0 153.5 jit_solution(17867262346764709764)
XLA Ops:
  0.0 1.3 select_reduce_fusion.slot_of
  1.3 149.9 %shard_map.100 = bf16[512,1024]{1,0:T(8,128)(2,1)} custom-call(s32[64]{0:T(128)} %block_of.1, s32[64]{0:T(128)} %select_reduce_fusion.slot_of, s32[256,1,128]{2,1,0:T(1,128)} %bitcast.4, f32[1,128]{1,0:T(1,128)} %constant.68.freqs, bf16[128,5120]{1,0:T(8,128)(2,1)} %tok.1, f32[1,5120]{1,0:T(1,128)} %bitcast.5, bf16[80,1024]{1,0:T(8,128)(2,1)} %wq.1, ...), custom_call_target="tpu_custom_call" | custom-call | flops 6710886400 | bytes 10485760 | tf_op jit(solution)/shard_map/pallas_call | solution.py:726
  151.2 2.3 %copy.12 = bf16[512,1024]{1,0:T(8,128)(2,1)} copy(bf16[512,1024]{1,0:T(8,128)(2,1)} %shard_map.100) | data formatting | bytes 2097152
  (1 shorter events, 0.0 us)
